TPU v7x, 32 devices: a whole 2x2x4 slice. The times are simulated.
32 devices in a mesh: dp: 8 (over z, core), chan: 4 (over y, x).
Axes of the slice: x: 2, y: 2, z: 4, core: 2. Of those that a mesh axis runs over, the one named last changes fastest.
Arguments:
- feat_in: bfloat16 [512, 32, 1024], P('chan', 'dp'), may hold values from -6 to 6
- rgb_in: float32 [32, 3, 1024], P('dp'), may hold values from -6 to 6
- latent: float32 [32, 512], P('dp'), may hold values from -6 to 6
- noise_first: float32 [32, 4096], P('dp'), may hold values from -6 to 6
- noise_second: float32 [32, 4096], P('dp'), may hold values from -6 to 6
- live_count: int32 [8], P('dp'), may hold values from 1 to 4, 24 in all
- conv_first: bfloat16 [9, 512, 512], P(None, 'chan'), may hold values from -0.09375 to 0.09375
- conv_second: bfloat16 [9, 512, 512], P(None, 'chan'), may hold values from -0.09375 to 0.09375
- style_weight: float32 [3, 512, 512], P(None, None, 'chan'), may hold values from -0.25 to 0.25
- style_bias: float32 [3, 512], P(None, 'chan'), may hold values from 0.5 to 1.5
- rgb_weight: bfloat16 [3, 512], P(None, 'chan'), may hold values from -0.25 to 0.25
- conv_bias: float32 [2, 512], P(None, 'chan'), may hold values from -3 to 3
- rgb_bias: float32 [3], replicated, may hold values from -3 to 3
- noise_gain: float32 [2], replicated, may hold values from 0.2 to 1
- feat_grad: bfloat16 [512, 32, 4096], P('chan', 'dp'), may hold values from -6 to 6
- rgb_grad: float32 [32, 3, 4096], P('dp'), may hold values from -6 to 6
Outputs:
- feat_out: bfloat16 [512, 32, 4096], P('chan', 'dp')
- rgb_out: float32 [32, 3, 4096], P('dp', None, 'chan')
- feat_in_grad: float32 [512, 32, 1024], P('chan', 'dp')
- rgb_in_grad: float32 [32, 3, 1024], P('dp')
- latent_grad: float32 [32, 512], P('dp')
- conv_first_grad: float32 [9, 512, 512], P(None, 'chan')
- conv_second_grad: float32 [9, 512, 512], P(None, 'chan')
- style_weight_grad: float32 [3, 512, 512], P(None, None, 'chan')
- style_bias_grad: float32 [3, 512], P(None, 'chan')
- rgb_weight_grad: float32 [3, 512], P(None, 'chan')
- conv_bias_grad: float32 [2, 512], P(None, 'chan')
- rgb_bias_grad: float32 [3], replicated
- noise_gain_grad: float32 [2], replicated
Inputs may be any that keep to these rules, and one draw needn't show every extreme that they name: Shard s holds images in its first live_count[s] slots of 4; its other slots are empty. The counts add up to 24, and some shard is full.
All inputs are finite; a program needn't handle non-finite values.
Results may differ from a plain program's by a relative error of at most 0.0059.
Values may be sent and summed in bfloat16 or wider, within the bound.
A program may use at most 320 MiB of HBM per device.

v0:
```python
import functools

import jax
import jax.numpy as jnp
from jax import lax
from jax.experimental import pallas as pl
from jax.experimental.pallas import tpu as pltpu
from jax.sharding import PartitionSpec as P

SIDE = 64
HALF = 32


precise = lax.Precision.HIGHEST
epsilon = 1e-08
root_two = 1.4142135623730951
phase_taps = (((1, 0),), ((2, 0), (0, 1)))
phase_pairs = ((0, 0), (0, 1), (1, 0), (1, 1))


def leaky_silu(value):
    return root_two * (0.2 * value + 0.8 * jax.nn.silu(value))


def leaky_slope(value):
    sigma = jax.nn.sigmoid(value)
    return root_two * (0.2 + 0.8 * sigma * (1.0 + value * (1.0 - sigma)))


def shifted(field, row_shift, col_shift, width):
    cells = field.shape[-1]
    offset = row_shift * width + col_shift
    if offset > 0:
        result = jnp.concatenate(
            [field[..., offset:], jnp.zeros(field.shape[:-1] + (offset,), field.dtype)], axis=-1
        )
    elif offset < 0:
        result = jnp.concatenate(
            [jnp.zeros(field.shape[:-1] + (-offset,), field.dtype), field[..., : cells + offset]],
            axis=-1,
        )
    else:
        result = field
    if col_shift != 0:
        column = jnp.arange(cells) % width
        inside = (column + col_shift >= 0) & (column + col_shift < width)
        result = jnp.where(inside, result, jnp.zeros((), field.dtype))
    return result


def upsample_matrix(half_side):
    rows_out = jnp.arange(2 * half_side)[:, None]
    cols_in = jnp.arange(half_side)[None, :]
    centre = rows_out // 2
    beside = centre - 1 + 2 * (rows_out % 2)
    return (
        jnp.where(cols_in == centre, 0.75, 0.0) + jnp.where(cols_in == beside, 0.25, 0.0)
    ).astype(jnp.float32)


def alternate(phases, half_side):
    stacked = jnp.stack(phases)
    out_rows, batch_count = (stacked.shape[1], stacked.shape[2])
    blocked = stacked.reshape(2, 2, out_rows, batch_count, half_side, half_side)
    return blocked.transpose(2, 3, 4, 0, 5, 1).reshape(
        out_rows, batch_count, 4 * half_side * half_side
    )


def split_phases(field, half_side):
    out_rows, batch_count = (field.shape[0], field.shape[1])
    blocked = field.reshape(out_rows, batch_count, half_side, 2, half_side, 2)
    return [
        blocked[:, :, :, row_phase, :, col_phase].reshape(
            out_rows, batch_count, half_side * half_side
        )
        for row_phase, col_phase in phase_pairs
    ]


def up_conv(inputs, weight, half_side):
    shifted_inputs = {}
    for row_shift in (0, 1):
        for col_shift in (0, 1):
            shifted_inputs[row_shift, col_shift] = shifted(inputs, row_shift, col_shift, half_side)
    phases = []
    for row_phase, col_phase in phase_pairs:
        summed = None
        for row_tap, row_shift in phase_taps[row_phase]:
            for col_tap, col_shift in phase_taps[col_phase]:
                product = jnp.einsum(
                    "oc,cbp->obp",
                    weight[row_tap * 3 + col_tap],
                    shifted_inputs[row_shift, col_shift],
                    preferred_element_type=jnp.float32,
                )
                summed = product if summed is None else summed + product
        phases.append(summed)
    return alternate(phases, half_side)


def phase_grads(grad_field, half_side):
    grad_phases = split_phases(grad_field, half_side)
    shifted_grads = [None] * 9
    for phase_index in range(4):
        row_phase, col_phase = phase_pairs[phase_index]
        for row_tap, row_shift in phase_taps[row_phase]:
            for col_tap, col_shift in phase_taps[col_phase]:
                shifted_grads[row_tap * 3 + col_tap] = shifted(
                    grad_phases[phase_index], -row_shift, -col_shift, half_side
                )
    return shifted_grads


def flat_conv(inputs, weight, width):
    summed = None
    for tap_index in range(9):
        product = jnp.einsum(
            "oc,cbp->obp", weight[tap_index], inputs, preferred_element_type=jnp.float32
        )
        product = shifted(product, tap_index // 3 - 1, tap_index % 3 - 1, width)
        summed = product if summed is None else summed + product
    return summed


def body(
    feat_in,
    rgb_in,
    latent,
    noise_first,
    noise_second,
    live_count,
    conv_first,
    conv_second,
    style_weight,
    style_bias,
    rgb_weight,
    conv_bias,
    rgb_bias,
    noise_gain,
    feat_grad,
    rgb_grad,
):
    local_ch, images, half_pix = feat_in.shape
    pixels = feat_grad.shape[2]
    half_side = HALF
    full_side = SIDE
    chan_rank = lax.axis_index("chan")
    live_mask = (jnp.arange(images) < live_count[0]).astype(jnp.float32)
    styles = (
        jnp.einsum("bw,jwc->jbc", latent, style_weight, precision=precise) + style_bias[:, None, :]
    )
    first_all, second_all = (
        lax.all_gather(styles[0], "chan", axis=1, tiled=True),
        lax.all_gather(styles[1], "chan", axis=1, tiled=True),
    )
    weight_one = conv_first.astype(jnp.float32)
    weight_two = conv_second.astype(jnp.float32)
    squares_one = jnp.sum(weight_one * weight_one, axis=0)
    squares_two = jnp.sum(weight_two * weight_two, axis=0)
    demod_one = lax.rsqrt(
        jnp.dot(first_all * first_all, squares_one.T, precision=precise) + epsilon
    )
    demod_two = lax.rsqrt(
        jnp.dot(second_all * second_all, squares_two.T, precision=precise) + epsilon
    )
    scaled_one = (feat_in.astype(jnp.float32) * styles[0].T[:, :, None]).astype(jnp.bfloat16)
    gathered_one = lax.all_gather(scaled_one, "chan", axis=0, tiled=True)
    raised = up_conv(gathered_one, conv_first, half_side)
    pre_one = (
        raised * demod_one.T[:, :, None]
        + noise_gain[0] * noise_first[None, :, :]
        + conv_bias[0][:, None, None]
    )
    act_one = leaky_silu(pre_one)
    scaled_two = (act_one * styles[1].T[:, :, None]).astype(jnp.bfloat16)
    gathered_two = lax.all_gather(scaled_two, "chan", axis=0, tiled=True)
    convolved = flat_conv(gathered_two, conv_second, full_side)
    pre_two = (
        convolved * demod_two.T[:, :, None]
        + noise_gain[1] * noise_second[None, :, :]
        + conv_bias[1][:, None, None]
    )
    act_two = leaky_silu(pre_two)
    feat_out = (act_two * live_mask[None, :, None]).astype(jnp.bfloat16)
    scaled_rgb = (act_two * styles[2].T[:, :, None]).astype(jnp.bfloat16)
    color_part = jnp.einsum(
        "ko,obp->bkp", rgb_weight, scaled_rgb, preferred_element_type=jnp.float32
    )
    color = lax.psum_scatter(color_part, "chan", scatter_dimension=2, tiled=True)
    shard_pix = color.shape[2]
    lift_matrix = upsample_matrix(half_side)
    skip_up = jnp.einsum(
        "up,bkpq,vq->bkuv",
        lift_matrix,
        rgb_in.reshape(images, 3, half_side, half_side),
        lift_matrix,
        precision=precise,
    ).reshape(images, 3, pixels)
    skip_mine = lax.dynamic_slice_in_dim(skip_up, chan_rank * shard_pix, shard_pix, 2)
    rgb_out = (color + rgb_bias[None, :, None] + skip_mine) * live_mask[:, None, None]
    rgb_cot = rgb_grad * live_mask[:, None, None]
    color_cot = rgb_cot.astype(jnp.bfloat16)
    rgb_in_grad = jnp.einsum(
        "up,bkuv,vq->bkpq",
        lift_matrix,
        rgb_cot.reshape(images, 3, full_side, full_side),
        lift_matrix,
        precision=precise,
    ).reshape(images, 3, half_pix)
    rgb_bias_part = jnp.sum(rgb_cot, axis=(0, 2))
    rgb_weight_part = jnp.einsum(
        "bkp,obp->ko", color_cot, scaled_rgb, preferred_element_type=jnp.float32
    )
    back_rgb = jnp.einsum("ko,bkp->obp", rgb_weight, color_cot, preferred_element_type=jnp.float32)
    style_rgb_grad = jnp.sum(back_rgb * act_two, axis=2).T
    grad_pre_two = (
        feat_grad.astype(jnp.float32) * live_mask[None, :, None]
        + back_rgb * styles[2].T[:, :, None]
    ) * leaky_slope(pre_two)
    cot_two = (grad_pre_two * demod_two.T[:, :, None]).astype(jnp.bfloat16)
    inner_two = (
        -0.5 * demod_two * demod_two * demod_two * jnp.sum(grad_pre_two * convolved, axis=2).T
    )
    taps_two = jnp.stack(
        [
            shifted(cot_two, 1 - tap_index // 3, 1 - tap_index % 3, full_side)
            for tap_index in range(9)
        ]
    )
    squares_two_grad = jnp.dot(inner_two.T, second_all * second_all, precision=precise)
    conv_two_grad = (
        jnp.einsum("tobp,cbp->toc", taps_two, gathered_two, preferred_element_type=jnp.float32)
        + 2.0 * weight_two * squares_two_grad[None]
    )
    style_two_demod = 2.0 * second_all * jnp.dot(inner_two, squares_two, precision=precise)
    columns = conv_second
    back_two = lax.psum_scatter(
        jnp.einsum("toc,tobp->cbp", columns, taps_two, preferred_element_type=jnp.float32),
        "chan",
        scatter_dimension=0,
        tiled=True,
    )
    style_two_conv = jnp.sum(back_two * act_one, axis=2).T
    grad_pre_one = back_two * styles[1].T[:, :, None] * leaky_slope(pre_one)
    cot_one = (grad_pre_one * demod_one.T[:, :, None]).astype(jnp.bfloat16)
    inner_one = -0.5 * demod_one * demod_one * demod_one * jnp.sum(grad_pre_one * raised, axis=2).T
    taps_one = jnp.stack(phase_grads(cot_one, half_side))
    squares_one_grad = jnp.dot(inner_one.T, first_all * first_all, precision=precise)
    conv_one_grad = (
        jnp.einsum("tobp,cbp->toc", taps_one, gathered_one, preferred_element_type=jnp.float32)
        + 2.0 * weight_one * squares_one_grad[None]
    )
    style_one_demod = 2.0 * first_all * jnp.dot(inner_one, squares_one, precision=precise)
    columns = conv_first
    back_one = lax.psum_scatter(
        jnp.einsum("toc,tobp->cbp", columns, taps_one, preferred_element_type=jnp.float32),
        "chan",
        scatter_dimension=0,
        tiled=True,
    )
    feat_in_grad = back_one * styles[0].T[:, :, None]
    style_one_conv = jnp.sum(back_one * feat_in.astype(jnp.float32), axis=2).T
    demod_one_sum, demod_two_sum = (
        lax.psum_scatter(style_one_demod, "chan", scatter_dimension=1, tiled=True),
        lax.psum_scatter(style_two_demod, "chan", scatter_dimension=1, tiled=True),
    )
    style_grads = jnp.stack(
        [style_one_conv + demod_one_sum, style_two_conv + demod_two_sum, style_rgb_grad]
    )
    latent_part = jnp.einsum("jbc,jwc->bw", style_grads, style_weight, precision=precise)
    gain_part = jnp.stack(
        [
            jnp.sum(grad_pre_one * noise_first[None, :, :]),
            jnp.sum(grad_pre_two * noise_second[None, :, :]),
        ]
    )
    latent_grad, gain_chan = lax.psum((latent_part, gain_part), "chan")
    style_weight_part = jnp.einsum("bw,jbc->jwc", latent, style_grads, precision=precise)
    style_bias_part = jnp.sum(style_grads, axis=1)
    conv_bias_part = jnp.stack(
        [jnp.sum(grad_pre_one, axis=(1, 2)), jnp.sum(grad_pre_two, axis=(1, 2))]
    )
    totals = lax.psum(
        (
            conv_one_grad,
            conv_two_grad,
            style_weight_part,
            style_bias_part,
            rgb_weight_part,
            conv_bias_part,
            rgb_bias_part,
            gain_chan,
        ),
        "dp",
    )
    return (feat_out, rgb_out, feat_in_grad, rgb_in_grad, latent_grad) + tuple(totals)


BF = jnp.bfloat16
F32 = jnp.float32
TILE = 256
ROWS = 16
ANY = pl.BlockSpec(memory_space=pl.ANY)
SMEM = pl.BlockSpec(memory_space=pltpu.SMEM)
LIMIT = 60 * 1024 * 1024


def whole(shape):
    return pl.BlockSpec(shape, lambda j: (0,) * len(shape))


def dot(a, b):
    return jnp.dot(a, b, preferred_element_type=F32)


def dot_nt(a, b):
    return lax.dot_general(a, b, (((1,), (1,)), ((), ())), preferred_element_type=F32)


def wide(column):
    return jnp.concatenate([column] * (TILE // 128), axis=1)


def move(field, row_shift, col_shift):
    offset = row_shift * HALF + col_shift
    if offset == 0:
        return field
    cells = field.shape[1]
    lane = lax.broadcasted_iota(jnp.int32, field.shape, 1)
    row, col = lane // HALF, lane % HALF
    inside = (row + row_shift >= 0) & (row + row_shift < HALF)
    inside = inside & (col + col_shift >= 0) & (col + col_shift < HALF)
    rolled = pltpu.roll(field.astype(F32), (-offset) % cells, 1)
    return jnp.where(inside, rolled, 0.0).astype(field.dtype)


def near(parity, step):
    other = (parity + step) % 2
    return other, (parity + step - other) // 2


def copy_index(phase, row_step, col_step):
    a, r = near(phase // 2, row_step)
    b, q = near(phase % 2, col_step)
    return ((a * 2 + b) * 2 + abs(r)) * 2 + abs(q)


def make_copies(source, copies):
    chunk = 32

    @pl.loop(0, source.shape[1] // chunk)
    def _(i):
        rows = pl.ds(pl.multiple_of(i * chunk, chunk), chunk)
        for phase in range(4):
            field = source[phase, rows, :]
            row_sign = 1 if phase // 2 == 0 else -1
            col_sign = 1 if phase % 2 == 0 else -1
            for r in (0, 1):
                for q in (0, 1):
                    copies[(phase * 2 + r) * 2 + q, rows, :] = move(
                        field, row_sign * r, col_sign * q
                    )


def demodulate(full, square_row, demod):
    chunk = 32

    @pl.loop(0, full.shape[1] // chunk)
    def _(i):
        rows = pl.ds(pl.multiple_of(i * chunk, chunk), chunk)
        total = None
        for t in range(9):
            value = full[t, rows, :].astype(F32)
            total = value * value if total is None else total + value * value
        total = jnp.sum(total * square_row, axis=1, keepdims=True)
        demod[rows, :] = jnp.broadcast_to(lax.rsqrt(total + epsilon), (chunk, 128))


def chan_peer(me, k):
    if k == 1:
        return me + 1 - 2 * (me % 2)
    return (me + 2) % 4 if k == 2 else 3 - me


def rows_of(base, size):
    return pl.ds(pl.multiple_of(base, size), size)


def take_rows(packs, rows_ref, cols):
    for d in range(4):
        here = slice(d * 128, (d + 1) * 128)
        pack = packs[d]
        rows_ref[:, here] = pack
        for j in range(3, 8):
            cols[j - 3, here, :] = jnp.broadcast_to(pack[j : j + 1, :], (128, 128)).T


def take_phases(plain, order, stacked, noise, color_phases):
    lanes = 512
    for n in range(plain.shape[1] // lanes):
        here = slice(n * lanes, (n + 1) * lanes)
        value = plain[:, here]
        first = value.astype(BF)
        rest = value - first.astype(F32)
        second = rest.astype(BF)
        third = rest - second.astype(F32)
        part = jnp.concatenate([first.astype(F32), second.astype(F32)], axis=0).astype(BF)
        stacked[:, here] = part
        high = dot(part, order[...])
        low = dot(jnp.concatenate([third, third], axis=0).astype(BF), order[...])
        for phase in range(4):
            grouped = slice(phase * 128, (phase + 1) * 128)
            out = slice(n * 128, (n + 1) * 128)
            color_phases[phase, :, out] = high[:, grouped].astype(BF)
            for i in (0, 1):
                noise[4 * i + phase : 4 * i + phase + 1, out] = (
                    high[3 + i : 4 + i, grouped] + high[11 + i : 12 + i, grouped] + low[3 + i : 4 + i, grouped]
                )


def forward_kernel(gains, pack, x_in, own1, own2, feat_grad, plain, order_back, order,
                   raised_out, scaled_out, conv_out, feat_out, full1_out, full2_out, grad_out,
                   x_all, scaled_one, demod1, demod2, color, rgb_grad, cols, rows_ref, noise, color_phases,
                   raised, scaled, full1, full2, copies, conv_tile, feat_tile, ordered, packs, stacked,
                   load_sem, store_sem, tile_sem, pack_send, pack_recv, x_send, x_recv,
                   w_send, w_recv, swap_send, swap_recv, grad_send, grad_recv):
    me = lax.axis_index("chan")
    row = lax.axis_index("dp")
    core = row % 2
    twin = row + 1 - 2 * core
    mesh_id = pl.DeviceIdType.MESH
    chans = [me] + [chan_peer(me, k) for k in (1, 2, 3)]
    barrier = pltpu.get_barrier_semaphore()
    for k in (1, 2, 3):
        pl.semaphore_signal(barrier, inc=1, device_id={"chan": chans[k]}, device_id_type=mesh_id)
    pl.semaphore_signal(barrier, inc=1, device_id={"dp": twin}, device_id_type=mesh_id)
    pl.semaphore_wait(barrier, 4)

    def remote(source, target, sent, received, where):
        return pltpu.make_async_remote_copy(source, target, sent, received, device_id=where, device_id_type=mesh_id)

    pack_moves = [
        remote(pack.at[chans[k]], packs.at[me], pack_send.at[k - 1], pack_recv.at[k - 1], {"chan": chans[k]})
        for k in (1, 2, 3)
    ]
    x_moves = [
        remote(x_in.at[chans[k]], x_all.at[rows_of(me * 128, 128), :], x_send.at[k - 1], x_recv.at[k - 1],
               {"chan": chans[k]})
        for k in (1, 2, 3)
    ]
    for item in pack_moves + x_moves:
        item.start()

    def half_rows(k):
        return rows_of(chans[k] * 128 + core * 64, 64)

    fulls, owns = (full1, full2), (own1, own2)
    cut = 5

    def near_move(c, k):
        return remote(owns[c].at[:, rows_of(core * 64, 64), :], fulls[c].at[:, half_rows(0), :],
                      w_send.at[c, k - 1], w_recv.at[c, k - 1], {"chan": chans[k]})

    def relay_move(c, k):
        part = fulls[c].at[pl.ds(0, cut) if k == 1 else pl.ds(cut, 9 - cut), half_rows(k), :]
        return remote(part, part, w_send.at[c, 1 + k], w_recv.at[c, 1 + k], {"chan": chans[3 - k]})

    def swap_move(c, k):
        part = fulls[c].at[:, half_rows(k), :]
        return remote(part, part, swap_send.at[c, k - 1], swap_recv.at[c, k - 1], {"dp": twin})

    near = [[near_move(c, k) for k in (1, 2)] for c in (0, 1)]
    relay = [[relay_move(c, k) for k in (1, 2)] for c in (0, 1)]
    swap = [[swap_move(c, k) for k in (1, 2, 3)] for c in (0, 1)]

    for item in near[0]:
        item.start()
    loads = [
        pltpu.make_async_copy(pack.at[me], packs.at[me], load_sem.at[0]),
        pltpu.make_async_copy(x_in.at[me], x_all.at[rows_of(me * 128, 128), :], load_sem.at[1]),
        pltpu.make_async_copy(own1, full1.at[:, rows_of(me * 128, 128), :], load_sem.at[2]),
        pltpu.make_async_copy(own2, full2.at[:, rows_of(me * 128, 128), :], load_sem.at[3]),
    ]
    for item in loads:
        item.start()
    take_phases(plain, order_back, stacked, noise, color_phases)
    loads[0].wait()
    for item in pack_moves:
        item.wait_recv()
    take_rows(packs, rows_ref, cols)
    loads[1].wait()
    for item in x_moves:
        item.wait_recv()

    @pl.loop(0, x_all.shape[0] // 32)
    def _(i):
        rows = rows_of(i * 32, 32)
        style = jnp.concatenate([cols[0, rows, :]] * 8, axis=1)
        value = (x_all[rows, :].astype(F32) * style).astype(BF)
        scaled_one[rows, :] = value
        for r in (0, 1):
            for q in (0, 1):
                copies[2 * r + q, rows, :] = move(value, r, q)

    for k in (0, 1):
        near[0][k].wait_recv()
        relay[0][k].start()
        swap[0][k].start()
    for item in near[1]:
        item.start()
    for item in relay[0]:
        item.wait_recv()
    swap[0][2].start()
    loads[2].wait()
    for item in swap[0]:
        item.wait_recv()
    store1 = pltpu.make_async_copy(full1, full1_out, store_sem.at[0])
    store1.start()
    demodulate(full1, rows_ref[3:4, :] * rows_ref[3:4, :], demod1)

    grad_moves = [
        remote(feat_grad.at[chans[k]], grad_out.at[rows_of(me * 128, 128), :], grad_send.at[k - 1], grad_recv.at[k - 1],
               {"chan": chans[k]})
        for k in (1, 2, 3)
    ]
    local3 = pltpu.make_async_copy(feat_grad.at[me], grad_out.at[rows_of(me * 128, 128), :], store_sem.at[4])

    @pl.loop(0, raised.shape[2] // TILE)
    def _(j):
        here = rows_of(j * TILE, TILE)
        for phase, (row_phase, col_phase) in enumerate(phase_pairs):
            total = None
            for k, r in phase_taps[row_phase]:
                for l, q in phase_taps[col_phase]:
                    term = dot(full1[3 * k + l], copies[2 * r + q, :, here])
                    total = term if total is None else total + term
            raised[phase, :, here] = total
            noise_row = gains[0] * noise[phase : phase + 1, here]
            for i in range(raised.shape[1] // ROWS):
                rows = slice(i * ROWS, (i + 1) * ROWS)
                pre = raised[phase, rows, here] * wide(demod1[rows, :]) + noise_row + wide(cols[3, rows, :])
                act = pre * (0.6 * root_two + 0.4 * root_two * jnp.tanh(0.5 * pre))
                scaled[phase, rows, here] = (act * wide(cols[1, rows, :])).astype(BF)

        @pl.when(j == 1)
        def _():
            for k in (0, 1):
                near[1][k].wait_recv()
                relay[1][k].start()
                swap[1][k].start()
            for item in grad_moves:
                item.start()
            local3.start()

    stores = [
        pltpu.make_async_copy(raised, raised_out, store_sem.at[1]),
        pltpu.make_async_copy(scaled, scaled_out, store_sem.at[2]),
    ]
    for item in stores:
        item.start()
    make_copies(scaled, copies)
    for item in relay[1]:
        item.wait_recv()
    swap[1][2].start()
    loads[3].wait()
    for item in swap[1]:
        item.wait_recv()
    store2 = pltpu.make_async_copy(full2, full2_out, store_sem.at[3])
    store2.start()
    demodulate(full2, rows_ref[4:5, :] * rows_ref[4:5, :], demod2)
    rgb_rows = jnp.concatenate([rows_ref[...] * rows_ref[5:6, :]] * 2, axis=0).astype(BF)
    live = gains[2]
    rgb_grad[...] = jnp.zeros_like(rgb_grad)

    def tile_stores(j, slot):
        return (
            pltpu.make_async_copy(conv_tile.at[slot], conv_out.at[:, :, rows_of(j * TILE, TILE)], tile_sem.at[0, slot]),
            pltpu.make_async_copy(feat_tile.at[slot], feat_out.at[:, rows_of(j * 4 * TILE, 4 * TILE)], tile_sem.at[1, slot]),
        )

    @pl.loop(0, raised.shape[2] // TILE)
    def _(j):
        here = rows_of(j * TILE, TILE)
        slot = j % 2

        @pl.when(j >= 2)
        def _():
            for item in tile_stores(j - 2, slot):
                item.wait()

        for phase in range(4):
            total = None
            for t in range(9):
                term = dot(full2[t], copies[copy_index(phase, t // 3 - 1, t % 3 - 1), :, here])
                total = term if total is None else total + term
            conv_tile[slot, phase] = total
            noise_row = gains[1] * noise[4 + phase : 5 + phase, here]
            for i in range(raised.shape[1] // ROWS):
                rows = slice(i * ROWS, (i + 1) * ROWS)
                pre = conv_tile[slot, phase, rows, :] * wide(demod2[rows, :]) + noise_row + wide(cols[4, rows, :])
                act = pre * (0.6 * root_two + 0.4 * root_two * jnp.tanh(0.5 * pre))
                out = (act * live).astype(BF)
                for half in range(TILE // 128):
                    ordered[half, rows, phase * 128 : (phase + 1) * 128] = out[:, half * 128 : (half + 1) * 128]
        for half in range(TILE // 128):
            image = dot(ordered[half], order[...]).astype(BF)
            feat_tile[slot, :, half * 512 : (half + 1) * 512] = image
            pixels = rows_of(j * 4 * TILE + half * 512, 512)
            color[:, pixels] = dot(rgb_rows, image)
            rgb_grad[...] += dot_nt(stacked[:, pixels], image)
        for item in tile_stores(j, slot):
            item.start()

    for j in (2, 3):
        for item in tile_stores(j, j % 2):
            item.wait()
    for item in [store1, store2, local3] + stores:
        item.wait()
    for item in pack_moves + x_moves + near[0] + near[1] + relay[0] + relay[1] + swap[0] + swap[1]:
        item.wait_send()
    for item in grad_moves:
        item.wait()


def backward_kernel(gains, arrived, convolved, raised, scaled_two, full1, full2, feat_natural,
                    scaled_one, x_all, cols, rows_ref, demod1, demod2, noise, order, color_phases, rgb_grad,
                    style_weight, shared, color,
                    feat_all, back_all, grad1_out, grad2_out, every, every_shared, latent_grad, color_in,
                    sums2, sums1, sums0, inner2, inner1, style_sums, vectors, owned, latent_in, tile, grad_tile, copies, field, weight, total, back,
                    keep, send, core1, core2, quad1, quad2, zsum1, zsum2, zin1, zin2, out1, out2,
                    load_sem, tile_sem, feat_send, feat_recv, back_send, back_recv, core_send, core_recv,
                    quad_send, quad_recv, z_send, z_recv, all_send, all_recv, twin_send, twin_recv,
                    shared_send, shared_recv, every_send, every_recv, owned_send, owned_recv, latent_send, latent_recv, color_send, color_recv):
    me = lax.axis_index("chan")
    row = lax.axis_index("dp")
    core = row % 2
    depth = row // 2
    twin = row + 1 - 2 * core
    mesh_id = pl.DeviceIdType.MESH
    chans = [me] + [chan_peer(me, k) for k in (1, 2, 3)]
    depths = [depth] + [chan_peer(depth, k) for k in (1, 2, 3)]
    barrier = pltpu.get_barrier_semaphore()
    for k in (1, 2, 3):
        pl.semaphore_signal(barrier, inc=1, device_id={"chan": chans[k]}, device_id_type=mesh_id)
    lines = [depths[k] * 2 + core for k in (1, 2, 3)] + [twin] + [depths[k] * 2 + 1 - core for k in (1, 2, 3)]
    for line in lines:
        pl.semaphore_signal(barrier, inc=1, device_id={"dp": line}, device_id_type=mesh_id)
    pl.semaphore_wait(barrier, 10)

    def remote(source, target, sent, received, where):
        return pltpu.make_async_remote_copy(source, target, sent, received, device_id=where, device_id_type=mesh_id)

    shared_moves = [
        remote(shared, every_shared.at[row], shared_send.at[i], shared_recv.at[i], {"dp": line})
        for i, line in enumerate(lines)
    ]
    for item in shared_moves:
        item.start()
    every_shared[row] = shared[...]

    quarter = color.shape[1] // 4
    color_moves = [
        remote(color.at[0:8, rows_of(chans[k] * quarter, quarter)], color_in.at[me],
               color_send.at[k - 1], color_recv.at[k - 1], {"chan": chans[k]})
        for k in (1, 2, 3)
    ]
    for item in color_moves:
        item.start()
    color_own = pltpu.make_async_copy(color.at[0:8, rows_of(me * quarter, quarter)], color_in.at[me], load_sem.at[9])
    color_own.start()

    feat_moves = [
        remote(feat_natural.at[rows_of(chans[k] * 128, 128), :], feat_all.at[me],
               feat_send.at[k - 1], feat_recv.at[k - 1], {"chan": chans[k]})
        for k in (1, 2, 3)
    ]
    for item in feat_moves:
        item.start()
    feat_own = pltpu.make_async_copy(feat_natural.at[rows_of(me * 128, 128), :], feat_all.at[me], load_sem.at[0])
    feat_own.start()
    load2 = pltpu.make_async_copy(full2, weight, load_sem.at[1])
    load2.start()
    load_field = pltpu.make_async_copy(scaled_two, field, load_sem.at[2])
    load_field.start()

    def tiles_in(source, j, slot):
        return pltpu.make_async_copy(source.at[:, :, rows_of(j * TILE, TILE)], tile.at[slot], tile_sem.at[0, slot])

    def grads_in(j, slot):
        return pltpu.make_async_copy(
            arrived.at[:, rows_of(j * 4 * TILE, 4 * TILE)], grad_tile.at[slot], tile_sem.at[1, slot]
        )

    tiles_in(convolved, 0, 0).start()
    grads_in(0, 0).start()
    live = gains[2]
    channels = cols.shape[1]
    tiles = copies.shape[2] // TILE
    sums2[...] = jnp.zeros_like(sums2)
    sums1[...] = jnp.zeros_like(sums1)
    style_sums[...] = jnp.zeros_like(style_sums)
    is_color = lax.broadcasted_iota(jnp.int32, (16, channels), 0) < 3
    rgb_rows = jnp.where(is_color, jnp.concatenate([rows_ref[...]] * 2, axis=0), 0.0).astype(BF)

    def add_sums(sums, rows, values):
        for n, value in enumerate(values):
            sums[n, rows, :] += value[:, :128] + value[:, 128:]

    @pl.loop(0, tiles)
    def _(j):
        slot = j % 2

        @pl.when(j + 1 < tiles)
        def _():
            tiles_in(convolved, j + 1, 1 - slot).start()
            grads_in(j + 1, 1 - slot).start()

        tiles_in(convolved, j, slot).wait()
        grads_in(j, slot).wait()
        here = rows_of(j * TILE, TILE)
        for half in range(TILE // 128):
            total[half] = dot(grad_tile[slot, :, half * 512 : (half + 1) * 512], order[...])
        for phase in range(4):
            noise_plain = noise[4 + phase : 5 + phase, here]
            noise_row = gains[1] * noise_plain
            back[phase % 2] = lax.dot_general(
                rgb_rows, color_phases[phase, :, here], (((0,), (0,)), ((), ())), preferred_element_type=F32
            )
            for i in range(channels // ROWS):
                rows = slice(i * ROWS, (i + 1) * ROWS)
                conv = tile[slot, phase, rows, :]
                scale = wide(demod2[rows, :])
                pre = conv * scale + noise_row + wide(cols[4, rows, :])
                sigma = 0.5 + 0.5 * jnp.tanh(0.5 * pre)
                slope = root_two * (0.2 + 0.8 * sigma * (1.0 + pre * (1.0 - sigma)))
                grad_feat = jnp.concatenate(
                    [total[half, rows, phase * 128 : (phase + 1) * 128] for half in range(TILE // 128)], axis=1
                )
                grad = (grad_feat * live + back[phase % 2, rows, :] * wide(cols[2, rows, :])) * slope
                copies[4 * phase, rows, here] = (grad * scale).astype(BF)
                add_sums(sums2, rows, (grad * conv, grad, grad * noise_plain))

    tiles_in(raised, 0, 0).start()
    late = [
        pltpu.make_async_copy(scaled_one, grad_tile.at[0], load_sem.at[4]),
        pltpu.make_async_copy(x_all, grad_tile.at[1], load_sem.at[5]),
    ]
    for item in late:
        item.start()

    def inner_of(sums, demod, inner):
        scale = demod[...]
        inner[...] = -0.5 * scale * scale * scale * jnp.sum(sums[0], axis=1, keepdims=True)

    inner_of(sums2, demod2, inner2)

    def spread_copies():
        chunk = 32

        @pl.loop(0, channels // chunk)
        def _(i):
            rows = rows_of(i * chunk, chunk)
            for phase in range(4):
                value = copies[4 * phase, rows, :]
                row_sign = 1 if phase // 2 == 0 else -1
                col_sign = 1 if phase % 2 == 0 else -1
                for r, q in ((0, 1), (1, 0), (1, 1)):
                    copies[4 * phase + 2 * r + q, rows, :] = move(value, row_sign * r, col_sign * q)

    spread_copies()
    load2.wait()
    load_field.wait()

    def split(c, slot, t, inner, square_row):
        for k in range(4):
            base = chans[k] * 128
            for out, start in ((keep, base + core * 64), (send, base + 64 - core * 64)):
                rows = rows_of(start, 64)
                column = jnp.concatenate([inner[rows, :]] * 4, axis=1)
                plain = weight[t, rows, :].astype(F32)
                scaled = plain * column
                out[t, k] = (total[slot, rows, :] + scaled * square_row).astype(BF)
                scaled = plain * scaled
                style_sums[c] += sum(scaled[i * 8 : (i + 1) * 8, :] for i in range(8))

    cores, quads, zsums, zins, outs = (core1, core2), (quad1, quad2), (zsum1, zsum2), (zin1, zin2), (out1, out2)

    def taps(g):
        return pl.ds(3 * g, 3)

    def core_move(c, g):
        return remote(send.at[taps(g)], cores[c].at[taps(g)], core_send.at[c, g], core_recv.at[c, g], {"dp": twin})

    def quad_move(c, g, k):
        return remote(keep.at[taps(g), k], quads[c].at[taps(g), k - 1], quad_send.at[c, g, k - 1],
                      quad_recv.at[c, g, k - 1], {"chan": chans[k]})

    def z_move(c, g, k):
        return remote(zsums[c].at[taps(g), rows_of(depths[k] * 16, 16), :], zins[c].at[taps(g), k - 1],
                      z_send.at[c, g, k - 1], z_recv.at[c, g, k - 1], {"dp": depths[k] * 2 + core})

    def all_move(c, g, k):
        part = outs[c].at[taps(g), rows_of(core * 64 + depth * 16, 16), :]
        return remote(part, part, all_send.at[c, g, k - 1], all_recv.at[c, g, k - 1], {"dp": depths[k] * 2 + core})

    def twin_move(c, g):
        part = outs[c].at[taps(g), rows_of(core * 64, 64), :]
        return remote(part, part, twin_send.at[c, g], twin_recv.at[c, g], {"dp": twin})

    def join_cores(c, g):
        core_move(c, g).wait_recv()
        for i in range(3):
            t = 3 * g + i
            for k in range(4):
                keep[t, k] = (keep[t, k].astype(F32) + cores[c][t, k].astype(F32)).astype(BF)
        for k in (1, 2, 3):
            quad_move(c, g, k).start()

    def join_quad(c, g):
        for k in (1, 2, 3):
            quad_move(c, g, k).wait_recv()
        for i in range(3):
            t = 3 * g + i
            value = keep[t, 0].astype(F32)
            for k in range(3):
                value = value + quads[c][t, k].astype(F32)
            zsums[c][t] = value.astype(BF)
        for k in (1, 2, 3):
            z_move(c, g, k).start()

    def join_depth(c, g):
        for k in (1, 2, 3):
            z_move(c, g, k).wait_recv()
        for i in range(3):
            t = 3 * g + i
            value = zsums[c][t, rows_of(depth * 16, 16), :].astype(F32)
            for k in range(3):
                value = value + zins[c][t, k].astype(F32)
            outs[c][t, rows_of(core * 64 + depth * 16, 16), :] = value.astype(BF)
        for k in (1, 2, 3):
            all_move(c, g, k).start()

    def join_all(c, g):
        for k in (1, 2, 3):
            all_move(c, g, k).wait_recv()
        twin_move(c, g).start()

    def weight_grad(c, product, inner, square_row):
        @pl.loop(0, 3)
        def _(g):
            t = 3 * g
            total[0] = product(t)
            total[1] = product(t + 1)
            split(c, 0, t, inner, square_row)
            total[0] = product(t + 2)
            split(c, 1, t + 1, inner, square_row)
            split(c, 0, t + 2, inner, square_row)
            core_move(c, g).start()

            @pl.when(g >= 1)
            def _():
                join_cores(c, g - 1)

        join_cores(c, 2)
        for g in range(3):
            core_move(c, g).wait_send()

    def second_product(t):
        row_step, col_step = 1 - t // 3, 1 - t % 3
        summed = None
        for phase in range(4):
            a, b = phase // 2, phase % 2
            far_row = (row_step * (2 * a - 1) + 1) // 2 * (row_step * row_step)
            far_col = (col_step * (2 * b - 1) + 1) // 2 * (col_step * col_step)
            index = (((a + row_step + 2) % 2 * 2 + (b + col_step + 2) % 2) * 2 + far_row) * 2 + far_col
            term = dot_nt(copies[index], field[phase])
            summed = term if summed is None else summed + term
        return summed

    weight_grad(1, second_product, inner2, 2.0 * rows_ref[4:5, :] * rows_ref[4:5, :])

    def turn():
        @pl.loop(0, 9)
        def _(t):
            weight[t] = weight[t].T

    turn()

    @pl.loop(0, tiles)
    def _(j):
        slot = j % 2

        @pl.when(j + 1 < tiles)
        def _():
            tiles_in(raised, j + 1, 1 - slot).start()

        tiles_in(raised, j, slot).wait()
        here = rows_of(j * TILE, TILE)
        for phase in range(4):
            summed = None
            for t in range(9):
                term = dot(weight[t], copies[copy_index(phase, 1 - t // 3, 1 - t % 3), :, here])
                summed = term if summed is None else summed + term
            back[phase % 2] = summed
            noise_plain = noise[phase : phase + 1, here]
            noise_row = gains[0] * noise_plain
            for i in range(channels // ROWS):
                rows = slice(i * ROWS, (i + 1) * ROWS)
                conv = tile[slot, phase, rows, :]
                scale = wide(demod1[rows, :])
                pre = conv * scale + noise_row + wide(cols[3, rows, :])
                sigma = 0.5 + 0.5 * jnp.tanh(0.5 * pre)
                act = root_two * (pre * (0.2 + 0.8 * sigma))
                slope = root_two * (0.2 + 0.8 * sigma * (1.0 + pre * (1.0 - sigma)))
                value = back[phase % 2, rows, :]
                grad = value * wide(cols[1, rows, :]) * slope
                field[phase, rows, here] = (grad * scale).astype(BF)
                add_sums(sums1, rows, (grad * conv, grad, grad * noise_plain, value * act))

        @pl.when(j == 2)
        def _():
            join_quad(1, 0)
            join_quad(1, 1)

    inner_of(sums1, demod1, inner1)
    load1 = pltpu.make_async_copy(full1, weight, load_sem.at[1])
    load1.start()

    @pl.loop(0, channels // 32)
    def _(i):
        rows = rows_of(i * 32, 32)
        for phase, (row_phase, col_phase) in enumerate(phase_pairs):
            value = field[phase, rows, :]
            for k, r in phase_taps[row_phase]:
                for l, q in phase_taps[col_phase]:
                    copies[3 * k + l, rows, :] = move(value, -r, -q)

    join_quad(1, 2)
    for g in range(3):
        for k in (1, 2, 3):
            quad_move(1, g, k).wait_send()
    load1.wait()
    for item in late:
        item.wait()
    weight_grad(0, lambda t: dot_nt(copies[t], grad_tile[0]), inner1, 2.0 * rows_ref[3:4, :] * rows_ref[3:4, :])
    style_loads = [
        pltpu.make_async_copy(style_weight.at[j], total.at[0, :, j * 128 : (j + 1) * 128], load_sem.at[6 + j])
        for j in range(3)
    ]
    for item in style_loads:
        item.start()
    for g in range(3):
        join_depth(1, g)
    turn()

    for n in range(tiles):
        here = slice(n * TILE, (n + 1) * TILE)
        summed = None
        for t in range(9):
            term = dot(weight[t], copies[t, :, here])
            summed = term if summed is None else summed + term
        back[n % 2] = summed
        for i in range(channels // ROWS):
            rows = slice(i * ROWS, (i + 1) * ROWS)
            value = back[n % 2, rows, :]
            copies[9, rows, here] = (value * wide(cols[0, rows, :])).astype(BF)
            item = value * grad_tile[1, rows, here].astype(F32)
            item = item[:, :128] + item[:, 128:]
            sums0[rows, :] = item if n == 0 else sums0[rows, :] + item
        if n == 1:
            join_quad(0, 0)
    back_moves = [
        remote(copies.at[9, rows_of(chans[k] * 128, 128), :], back_all.at[me],
               back_send.at[k - 1], back_recv.at[k - 1], {"chan": chans[k]})
        for k in (1, 2, 3)
    ]
    for item in back_moves:
        item.start()
    back_own = pltpu.make_async_copy(copies.at[9, rows_of(me * 128, 128), :], back_all.at[me], load_sem.at[2])
    back_own.start()

    def as_row(sums):
        return jnp.sum(sums[...].T, axis=0, keepdims=True)

    style_two, style_one = as_row(sums1.at[3]), as_row(sums0)
    color_grad = rgb_grad[0:8, :]
    vector_rows = [
        style_one + 2.0 * rows_ref[3:4, :] * jnp.sum(style_sums[0], axis=0, keepdims=True),
        style_two + 2.0 * rows_ref[4:5, :] * jnp.sum(style_sums[1], axis=0, keepdims=True),
        sum(rows_ref[k : k + 1, :] * color_grad[k : k + 1, :] for k in range(3)),
        as_row(sums1.at[1]),
        as_row(sums2.at[1]),
        jnp.broadcast_to(jnp.sum(as_row(sums1.at[2]), axis=1, keepdims=True), (1, channels)),
        jnp.broadcast_to(jnp.sum(as_row(sums2.at[2]), axis=1, keepdims=True), (1, channels)),
        jnp.zeros((1, channels), F32),
    ]
    for i, value in enumerate(vector_rows):
        for d in range(4):
            vectors[d, i : i + 1, :] = value[:, d * 128 : (d + 1) * 128]
    color_grad = color_grad * rows_ref[5:6, :]
    for d in range(4):
        vectors[d, 8:16, :] = color_grad[:, d * 128 : (d + 1) * 128]
    owned_moves = [
        remote(vectors.at[chans[k]], owned.at[me], owned_send.at[k - 1], owned_recv.at[k - 1], {"chan": chans[k]})
        for k in (1, 2, 3)
    ]
    for item in owned_moves:
        item.start()
    owned[me] = vectors[me]

    for g in range(3):
        join_all(1, g)
    join_quad(0, 1)
    join_depth(0, 0)
    for item in owned_moves:
        item.wait_recv()
    for item in style_loads:
        item.wait()
    latent_part = None
    for j in range(3):
        value = jnp.concatenate([owned[d, j : j + 1, :] for d in range(4)] + [jnp.zeros((4, 128), F32)], axis=0)
        term = lax.dot_general(
            value, total[0, :, j * 128 : (j + 1) * 128], (((1,), (1,)), ((), ())), precision=precise, preferred_element_type=F32
        )
        latent_part = term if latent_part is None else latent_part + term
    latent_in[3] = latent_part
    latent_moves = [
        remote(latent_in.at[3], latent_in.at[k - 1], latent_send.at[k - 1], latent_recv.at[k - 1], {"chan": chans[k]})
        for k in (1, 2, 3)
    ]
    every_moves = [
        remote(owned, every.at[row], every_send.at[i], every_recv.at[i], {"dp": line})
        for i, line in enumerate(lines)
    ]
    for item in latent_moves + every_moves:
        item.start()
    every[row] = owned[...]
    join_quad(0, 2)
    join_depth(0, 1)
    join_all(0, 0)
    join_depth(0, 2)
    join_all(0, 1)
    for g in range(3):
        twin_move(1, g).wait()
    store2 = pltpu.make_async_copy(out2, grad2_out, load_sem.at[1])
    store2.start()
    join_all(0, 2)
    for item in latent_moves:
        item.wait_recv()
    latent_grad[...] = latent_in[0] + latent_in[1] + latent_in[2] + latent_in[3]
    for g in range(3):
        twin_move(0, g).wait()
    store1 = pltpu.make_async_copy(out1, grad1_out, load_sem.at[3])
    store1.start()
    for c in (0, 1):
        for g in range(3):
            for k in (1, 2, 3):
                if c == 0:
                    quad_move(c, g, k).wait_send()
                z_move(c, g, k).wait_send()
                all_move(c, g, k).wait_send()
    for item in feat_moves + back_moves + shared_moves + every_moves + color_moves:
        item.wait()
    for item in owned_moves + latent_moves:
        item.wait_send()
    for item in (feat_own, back_own, color_own, store2, store1):
        item.wait()


def pick(value, index, axis):
    return lax.dynamic_index_in_dim(value, index, axis, keepdims=False)


def phase_order():
    place = jnp.arange(512)
    row, col = place // SIDE, place % SIDE
    grouped = ((row % 2) * 2 + col % 2) * 128 + (row // 2) * HALF + col // 2
    return (jnp.arange(512)[:, None] == grouped[None, :]).astype(BF)


def image_body(
    feat_in,
    rgb_in,
    latent,
    noise_first,
    noise_second,
    live_count,
    conv_first,
    conv_second,
    style_weight,
    style_bias,
    rgb_weight,
    conv_bias,
    rgb_bias,
    noise_gain,
    feat_grad,
    rgb_grad,
):
    local_ch, images, half_pix = feat_in.shape
    channels = 4 * local_ch
    pixels = feat_grad.shape[2]
    me = lax.axis_index("chan")
    live_mask = (jnp.arange(images) < live_count[0]).astype(F32)
    live = (me < live_count[0]).astype(F32)
    gains = jnp.concatenate([noise_gain, live[None]])
    styles = jnp.einsum("bw,jwc->bjc", latent, style_weight, precision=precise) + style_bias[None]

    def each_image(value):
        return jnp.broadcast_to(value[None], (images,) + value.shape)

    pack = jnp.concatenate([each_image(rgb_weight.astype(F32)), styles, each_image(conv_bias)], axis=1)
    plain = jnp.concatenate(
        [pick(rgb_grad, me, 0) * live, pick(noise_first, me, 0)[None], pick(noise_second, me, 0)[None],
         jnp.zeros((3, pixels), F32)]
    )
    x_by_image = feat_in.transpose(1, 0, 2)
    grad_by_image = feat_grad.transpose(1, 0, 2)
    order = phase_order()

    vmem = pl.BlockSpec(memory_space=pltpu.VMEM)
    field, wide_weight = (4, channels, half_pix), (9, channels, channels)
    vector = ((channels, 128), F32)
    forward_outs = (
        (field, F32), (field, BF), (field, F32), ((channels, pixels), BF), (wide_weight, BF), (wide_weight, BF),
        ((channels, pixels), BF), ((channels, half_pix), BF), ((channels, half_pix), BF), vector, vector,
        ((16, pixels), F32), ((16, channels), F32), ((5, channels, 128), F32), ((8, channels), F32),
        ((8, half_pix), F32), ((4, 16, half_pix), BF),
    )
    (raised, scaled_two, convolved, feat_natural, full_one, full_two, grad_arrived,
     x_all, scaled_one, demod_one, demod_two, color, rgb_part, cols, row_vectors, noise, color_phases) = pl.pallas_call(
        forward_kernel,
        in_specs=[SMEM, ANY, ANY, ANY, ANY, ANY, vmem, vmem, vmem],
        out_specs=[ANY] * 7 + [vmem] * 10,
        out_shape=[jax.ShapeDtypeStruct(shape, dtype) for shape, dtype in forward_outs],
        scratch_shapes=[
            pltpu.VMEM(field, F32),
            pltpu.VMEM(field, BF),
            pltpu.VMEM(wide_weight, BF),
            pltpu.VMEM(wide_weight, BF),
            pltpu.VMEM((16, channels, half_pix), BF),
            pltpu.VMEM((2, 4, channels, TILE), F32),
            pltpu.VMEM((2, channels, 4 * TILE), BF),
            pltpu.VMEM((TILE // 128, channels, 512), BF),
            pltpu.VMEM((4, 8, 128), F32),
            pltpu.VMEM((16, pixels), BF),
            pltpu.SemaphoreType.DMA((4,)),
            pltpu.SemaphoreType.DMA((5,)),
            pltpu.SemaphoreType.DMA((2, 2)),
        ]
        + [pltpu.SemaphoreType.DMA((3,))] * 4
        + [pltpu.SemaphoreType.DMA((2, 4))] * 2
        + [pltpu.SemaphoreType.DMA((2, 3))] * 2
        + [pltpu.SemaphoreType.DMA((3,))] * 2,
        compiler_params=pltpu.CompilerParams(vmem_limit_bytes=LIMIT, collective_id=0, has_side_effects=True),
        cost_estimate=pl.CostEstimate(flops=int(50e9), bytes_accessed=12 << 20, transcendentals=0),
    )(gains, pack, x_by_image, conv_first, conv_second, grad_by_image, plain, order.T, order)

    rgb_cot = rgb_grad * live_mask[:, None, None]
    rgb_bias_part = jnp.sum(rgb_cot, axis=(0, 2))
    shared = jnp.concatenate([latent, jnp.broadcast_to(jnp.pad(rgb_bias_part, (0, 509))[None], (4, 512))])
    backward_outs = (
        ((4, local_ch, pixels), BF), ((4, local_ch, half_pix), BF), ((9, local_ch, channels), BF),
        ((9, local_ch, channels), BF), ((8, 4, 16, 128), F32), ((8, 8, 512), F32), ((8, 512), F32),
        ((4, 8, pixels // 4), F32),
    )
    feat_all, back_all, grad_one, grad_two, every, every_shared, latent_grad, color_in = pl.pallas_call(
        backward_kernel,
        in_specs=[SMEM] + [ANY] * 9 + [vmem] * 8 + [ANY, vmem, ANY],
        out_specs=[ANY] * 4 + [vmem] * 3 + [ANY],
        out_shape=[jax.ShapeDtypeStruct(shape, dtype) for shape, dtype in backward_outs],
        scratch_shapes=[
            pltpu.VMEM((3, channels, 128), F32),
            pltpu.VMEM((4, channels, 128), F32),
            pltpu.VMEM((channels, 128), F32),
            pltpu.VMEM((channels, 128), F32),
            pltpu.VMEM((channels, 128), F32),
            pltpu.VMEM((2, 8, channels), F32),
            pltpu.VMEM((4, 16, 128), F32),
            pltpu.VMEM((4, 16, 128), F32),
            pltpu.VMEM((4, 8, 512), F32),
            pltpu.VMEM((2, 4, channels, TILE), F32),
            pltpu.VMEM((2, channels, 4 * TILE), BF),
            pltpu.VMEM((16, channels, half_pix), BF),
            pltpu.VMEM(field, BF),
            pltpu.VMEM(wide_weight, BF),
            pltpu.VMEM((2, channels, channels), F32),
            pltpu.VMEM((2, channels, TILE), F32),
        ]
        + [pltpu.VMEM((9, 4, 64, channels), BF)] * 4
        + [pltpu.VMEM((9, 3, 64, channels), BF)] * 2
        + [pltpu.VMEM((9, 64, channels), BF)] * 2
        + [pltpu.VMEM((9, 3, 16, channels), BF)] * 2
        + [pltpu.VMEM((9, local_ch, channels), BF)] * 2
        + [pltpu.SemaphoreType.DMA((10,)), pltpu.SemaphoreType.DMA((2, 2))]
        + [pltpu.SemaphoreType.DMA((3,))] * 4
        + [pltpu.SemaphoreType.DMA((2, 3))] * 2
        + [pltpu.SemaphoreType.DMA((2, 3, 3))] * 6
        + [pltpu.SemaphoreType.DMA((2, 3))] * 2
        + [pltpu.SemaphoreType.DMA((7,))] * 4
        + [pltpu.SemaphoreType.DMA((3,))] * 6,
        compiler_params=pltpu.CompilerParams(vmem_limit_bytes=LIMIT, collective_id=1, has_side_effects=True),
        cost_estimate=pl.CostEstimate(flops=int(100e9), bytes_accessed=12 << 20, transcendentals=0),
    )(gains, grad_arrived, convolved, raised, scaled_two, full_one, full_two, feat_natural, scaled_one, x_all,
      cols, row_vectors, demod_one, demod_two, noise, order.T, color_phases, rgb_part, style_weight, shared, color)
    feat_out = feat_all.transpose(1, 0, 2)
    feat_in_grad = back_all.transpose(1, 0, 2).astype(F32)
    grad_one, grad_two = grad_one.astype(F32), grad_two.astype(F32)

    lift_matrix = upsample_matrix(HALF)
    shard_pix = pixels // 4
    skip_up = jnp.einsum(
        "up,bkpq,vq->bkuv",
        lift_matrix,
        rgb_in.reshape(images, 3, HALF, HALF),
        lift_matrix,
        precision=precise,
    ).reshape(images, 3, pixels)
    skip_mine = lax.dynamic_slice_in_dim(skip_up, me * shard_pix, shard_pix, 2)
    rgb_out = (color_in[:, :3] + rgb_bias[None, :, None] + skip_mine) * live_mask[:, None, None]
    rgb_in_grad = jnp.einsum(
        "up,bkuv,vq->bkpq",
        lift_matrix,
        rgb_cot.reshape(images, 3, SIDE, SIDE),
        lift_matrix,
        precision=precise,
    ).reshape(images, 3, half_pix)

    summed = jnp.sum(every, axis=(0, 1))
    style_weight_grad = jnp.einsum("gbw,gbjc->jwc", every_shared[:, :4], every[:, :, :3], precision=precise)
    return (
        feat_out,
        rgb_out,
        feat_in_grad,
        rgb_in_grad,
        latent_grad[:4],
        grad_one,
        grad_two,
        style_weight_grad,
        summed[:3],
        summed[8:11],
        summed[3:5],
        jnp.sum(every_shared[:, 4, :3], axis=0),
        summed[5:7, 0],
    )


def solution(mesh):
    alone = mesh.shape["chan"] == 4 and mesh.shape["dp"] == 8
    return jax.shard_map(
        image_body if alone else body,
        mesh=mesh,
        in_specs=(
            P("chan", "dp", None),
            P("dp", None, None),
            P("dp", None),
            P("dp", None),
            P("dp", None),
            P("dp"),
            P(None, "chan", None),
            P(None, "chan", None),
            P(None, None, "chan"),
            P(None, "chan"),
            P(None, "chan"),
            P(None, "chan"),
            P(),
            P(),
            P("chan", "dp", None),
            P("dp", None, None),
        ),
        out_specs=(
            P("chan", "dp", None),
            P("dp", None, "chan"),
            P("chan", "dp", None),
            P("dp", None, None),
            P("dp", None),
            P(None, "chan", None),
            P(None, "chan", None),
            P(None, None, "chan"),
            P(None, "chan"),
            P(None, "chan"),
            P(None, "chan"),
            P(),
            P(),
        ),
        check_vma=False,
    )
```

profile of v0, /device:TPU:0, one launch (start us, length us, event | category | flops | bytes accessed | tf_op | source)
XLA Modules:
  0.0 302.3 jit_solution(8621667598929475394)
XLA Ops:
  1.4 1.2 pad_maximum_fusion.2.gains
  2.7 0.7 broadcast_in_dim.22
  3.4 1.6 fusion.18
  5.0 0.7 copy_add_fusion.1
  5.7 0.7 broadcast_in_dim.21
  7.0 0.9 constant_dynamic-slice_fusion.1
  7.9 1.0 constant_dynamic-slice_fusion.3
  9.0 0.7 maximum_maximum_fusion.plain
  9.7 0.9 reshape.186
  11.1 0.8 fusion.6
  12.8 1.1 fusion.74
  13.9 1.3 pad_maximum_fusion.1.shared
  16.1 0.8 reshape.189
  16.9 1.1 fusion.1
  18.0 1.3 copy.87
  19.3 6.5 %copy.86 = bf16[128,4,4096]{2,0,1:T(8,128)(2,1)} copy(bf16[128,4,4096]{2,1,0:T(4,128)(2,1)} %param.30) | data formatting | bytes 8388608 | tf_op args[14]
  25.8 106.1 %shard_map.255 = (f32[4,512,1024]{2,1,0:T(8,128)}, bf16[4,512,1024]{2,1,0:T(8,128)(2,1)}, f32[4,512,1024]{2,1,0:T(8,128)}, bf16[512,4096]{1,0:T(8,128)(2,1)}, bf...) custom-call(f32[3]{0:T(128)} %pad_maximum_fusion.2.gains, ...), custom_call_target="tpu_custom_call" | custom-call | flops 49999998976 | bytes 12582912 | tf_op jit(solution)/shard_map/pallas_call | solution.py:1131
  131.9 150.2 %shard_map.256 = (bf16[4,128,4096]{2,1,0:T(8,128)(2,1)}, bf16[4,128,1024]{2,1,0:T(8,128)(2,1)}, bf16[9,128,512]{2,1,0:T(8,128)(2,1)}, bf16[9,128,512]{2,1,0:T(8,...) custom-call(f32[3]{0:T(128)} %pad_maximum_fusion.2.gains, ...), custom_call_target="tpu_custom_call" | custom-call | flops 99999997952 | bytes 12582912 | tf_op jit(solution)/shard_map/pallas_call | solution.py:1167
  282.2 7.5 %copy.49 = bf16[128,4,4096]{2,1,0:T(4,128)(2,1)} copy(bf16[128,4,4096]{2,0,1:T(8,128)(2,1)} %bitcast.52) | data formatting | bytes 8388608
  293.4 0.8 convolution_bitcast_fusion
  294.3 1.1 copy.52
  295.7 2.7 copy.51
  298.4 1.7 convert_element_type.41
  300.1 1.7 convert_element_type.42
  (49 shorter events, 6.9 us)
Async XLA Ops:
  0.6 17.4 %copy-start.3 = (bf16[128,4,1024]{2,1,0:T(4,128)(2,1)S(1)}, bf16[128,4,1024]{2,1,0:T(4,128)(2,1)}, u32[]{:S(2)}) copy-start(bf16[128,4,1024]{2,1,0:T(4,128)(2,1)} %param.16) | copy-start | bytes 3145732
  2.6 16.7 %copy-start.8 = (f32[4]{0:T(128)}, f32[4]{0:T(128)S(1)}, u32[]{:S(2)}) copy-start(f32[4]{0:T(128)S(1)} %compare_convert_fusion) | copy-start | bytes 52
  282.1 7.6 %copy-start.11 = (f32[8,8,512]{2,1,0:T(8,128)S(1)}, f32[8,8,512]{2,1,0:T(8,128)}, u32[]{:S(2)}) copy-start(f32[8,8,512]{2,1,0:T(8,128)} %get-tuple-element.62) | copy-start | bytes 393220
  282.1 8.1 %copy-start.4 = (f32[8,4,16,128]{3,2,1,0:T(8,128)S(1)}, f32[8,4,16,128]{3,2,1,0:T(8,128)}, u32[]{:S(2)}) copy-start(f32[8,4,16,128]{3,2,1,0:T(8,128)} %get-tuple-element.61) | copy-start | bytes 786436
  282.1 9.9 %copy-start.7 = (f32[8,512]{1,0:T(8,128)S(1)}, f32[8,512]{1,0:T(8,128)}, u32[]{:S(2)}) copy-start(f32[8,512]{1,0:T(8,128)} %get-tuple-element.58) | copy-start | bytes 49156
  282.2 10.5 %copy-start.5 = (f32[4,3,1024]{2,0,1:T(4,128)S(1)}, f32[4,3,1024]{2,0,1:T(4,128)}, u32[]{:S(2)}) copy-start(f32[4,3,1024]{2,0,1:T(4,128)} %constant_dynamic-slice_fusion) | copy-start | bytes 147460
  282.2 10.5 %copy-start.6 = (f32[4,8,1024]{2,1,0:T(8,128)S(1)}, f32[4,8,1024]{2,1,0:T(8,128)}, u32[]{:S(2)}) copy-start(f32[4,8,1024]{2,1,0:T(8,128)} %get-tuple-element.56) | copy-start | bytes 393220
  282.2 10.5 %copy-start.9 = (f32[4]{0:T(128)S(1)}, f32[4]{0:T(128)}, u32[]{:S(2)}) copy-start(f32[4]{0:T(128)} %copy-done.8) | copy-start | bytes 52
  282.2 10.5 %copy-start.10 = (f32[3]{0:T(128)S(1)}, f32[3]{0:T(128)}, u32[]{:S(2)}) copy-start(f32[3]{0:T(128)} %param.28) | copy-start | bytes 40
  289.7 5.7 %copy-start.2 = (bf16[4,128,1024]{2,1,0:T(8,128)(2,1)S(1)}, bf16[4,128,1024]{2,1,0:T(8,128)(2,1)}, u32[]{:S(2)}) copy-start(bf16[4,128,1024]{2,1,0:T(8,128)(2,1)} %get-tuple-element.57) | copy-start | bytes 3145732
  294.3 4.1 %copy-start.1 = (bf16[9,128,512]{2,1,0:T(8,128)(2,1)S(1)}, bf16[9,128,512]{2,1,0:T(8,128)(2,1)}, u32[]{:S(2)}) copy-start(bf16[9,128,512]{2,1,0:T(8,128)(2,1)} %get-tuple-element.59) | copy-start | bytes 3538948
  295.7 4.4 %copy-start = (bf16[9,128,512]{2,1,0:T(8,128)(2,1)S(1)}, bf16[9,128,512]{2,1,0:T(8,128)(2,1)}, u32[]{:S(2)}) copy-start(bf16[9,128,512]{2,1,0:T(8,128)(2,1)} %get-tuple-element.60) | copy-start | bytes 3538948
where the time goes:
time: 308 us; the launch traced here: 302 us
  Pallas kernels  256 us (83%)
  local copies, waits for them, and re-layouts  28.2 us (9%)
  other arithmetic  11.3 us (4%)
  matrix products  4.4 us (1%)
    pallas_call x1, Pallas kernels, image_body(): pl.pallas_call(backward_kernel, in_specs=[SMEM] + [ANY] * 9 + [vmem] * 8...  150 us
    pallas_call x1, Pallas kernels, image_body(): pl.pallas_call(forward_kernel, in_specs=[SMEM, ANY, ANY, ANY, ANY, ANY, v...  106 us
    unnamed x30, local copies, waits for them, and re-layouts  19.8 us

commit v1 on v0

--- a/solution.py
+++ b/solution.py
@@ -419,27 +419,39 @@
                 )
 
 
-def forward_kernel(gains, pack, x_in, own1, own2, feat_grad, plain, order_back, order,
-                   raised_out, scaled_out, conv_out, feat_out, full1_out, full2_out, grad_out,
-                   x_all, scaled_one, demod1, demod2, color, rgb_grad, cols, rows_ref, noise, color_phases,
-                   raised, scaled, full1, full2, copies, conv_tile, feat_tile, ordered, packs, stacked,
-                   load_sem, store_sem, tile_sem, pack_send, pack_recv, x_send, x_recv,
-                   w_send, w_recv, swap_send, swap_recv, grad_send, grad_recv):
+def block_kernel(gains, pack, x_in, own1, own2, feat_grad, plain, order_back, order, style_weight, shared,
+                 raised_out, conv_out, feat_natural, full1_out, arrived, x_out, scaled_one_out, by_image, feat_all,
+                 feat_out, back_all, grad1_out, grad2_out, color_in, every, every_shared, latent_grad,
+                 demod1, demod2, color, rgb_grad, cols, rows_ref, noise, color_phases, packs, stacked,
+                 full1, full2, copies, tile, grad_tile, field, total, back,
+                 core1, core2, first1, first2, quad1, quad2, zsum1, zsum2, zin1, zin2, out1, out2,
+                 sums2, sums1, sums0, inner2, inner1, style_sums, vectors, owned, latent_in, raw,
+                 load_sem, store_sem, tile_sem, pack_send, pack_recv, x_send, x_recv, w_send, w_recv,
+                 swap_send, swap_recv, grad_send, grad_recv, feat_send, feat_recv, back_send, back_recv,
+                 core_send, core_recv, quad_send, quad_recv, z_send, z_recv, across_send, across_recv, twin_send, twin_recv,
+                 first_send, first_recv, beside_send, beside_recv,
+                 shared_send, shared_recv, every_send, every_recv, owned_send, owned_recv, latent_send, latent_recv,
+                 color_send, color_recv, raw_sem, image_sem):
     me = lax.axis_index("chan")
     row = lax.axis_index("dp")
     core = row % 2
+    depth = row // 2
     twin = row + 1 - 2 * core
     mesh_id = pl.DeviceIdType.MESH
     chans = [me] + [chan_peer(me, k) for k in (1, 2, 3)]
+    depths = [depth] + [chan_peer(depth, k) for k in (1, 2, 3)]
+    lines = [depths[k] * 2 + core for k in (1, 2, 3)] + [twin] + [depths[k] * 2 + 1 - core for k in (1, 2, 3)]
     barrier = pltpu.get_barrier_semaphore()
     for k in (1, 2, 3):
         pl.semaphore_signal(barrier, inc=1, device_id={"chan": chans[k]}, device_id_type=mesh_id)
-    pl.semaphore_signal(barrier, inc=1, device_id={"dp": twin}, device_id_type=mesh_id)
-    pl.semaphore_wait(barrier, 4)
+    for line in lines:
+        pl.semaphore_signal(barrier, inc=1, device_id={"dp": line}, device_id_type=mesh_id)
+    pl.semaphore_wait(barrier, 10)
 
     def remote(source, target, sent, received, where):
         return pltpu.make_async_remote_copy(source, target, sent, received, device_id=where, device_id_type=mesh_id)
 
+    x_all, scaled_one, scaled = grad_tile.at[1], grad_tile.at[0], field
     pack_moves = [
         remote(pack.at[chans[k]], packs.at[me], pack_send.at[k - 1], pack_recv.at[k - 1], {"chan": chans[k]})
         for k in (1, 2, 3)
@@ -484,7 +496,37 @@
     ]
     for item in loads:
         item.start()
+
+    def raw_in(n):
+        return pltpu.make_async_copy(
+            feat_grad.at[:, :, n * 512 : (n + 1) * 512], raw.at[n % 2], raw_sem.at[n % 2]
+        )
+
+    def image_store(n, half):
+        return pltpu.make_async_copy(
+            core1.at[n % 4 * 2 + half], by_image.at[half * 256 : (half + 1) * 256, n * 512 : (n + 1) * 512],
+            image_sem.at[n % 4, half],
+        )
+
+    raw_in(0).start()
+    raw_in(1).start()
     take_phases(plain, order_back, stacked, noise, color_phases)
+    for n in range(8):
+        if n >= 4:
+            image_store(n - 4, 0).wait()
+            image_store(n - 4, 1).wait()
+        raw_in(n).wait()
+
+        @pl.loop(0, 8)
+        def _(i):
+            value = jnp.swapaxes(raw[n % 2, rows_of(i * 16, 16), :, :], 0, 1)
+            for image in range(4):
+                core1[n % 4 * 2 + image // 2, rows_of(image % 2 * 128 + i * 16, 16), :] = value[image]
+
+        image_store(n, 0).start()
+        image_store(n, 1).start()
+        if n + 2 < 8:
+            raw_in(n + 2).start()
     loads[0].wait()
     for item in pack_moves:
         item.wait_recv()
@@ -519,29 +561,53 @@
     store1.start()
     demodulate(full1, rows_ref[3:4, :] * rows_ref[3:4, :], demod1)
 
-    grad_moves = [
-        remote(feat_grad.at[chans[k]], grad_out.at[rows_of(me * 128, 128), :], grad_send.at[k - 1], grad_recv.at[k - 1],
-               {"chan": chans[k]})
-        for k in (1, 2, 3)
-    ]
-    local3 = pltpu.make_async_copy(feat_grad.at[me], grad_out.at[rows_of(me * 128, 128), :], store_sem.at[4])
-
-    @pl.loop(0, raised.shape[2] // TILE)
+    def part_of(j):
+        return rows_of(j * 4 * TILE, 4 * TILE)
+
+    def grad_move(j, k):
+        return remote(by_image.at[rows_of(chans[k] * 128, 128), part_of(j)], arrived.at[rows_of(me * 128, 128), part_of(j)],
+                      grad_send.at[j, k - 1], grad_recv.at[j, k - 1], {"chan": chans[k]})
+
+    for n in range(4, 8):
+        image_store(n, 0).wait()
+        image_store(n, 1).wait()
+    local3 = pltpu.make_async_copy(by_image.at[rows_of(me * 128, 128), :], arrived.at[rows_of(me * 128, 128), :], store_sem.at[4])
+    stores = [
+        pltpu.make_async_copy(x_all, x_out, store_sem.at[1]),
+        pltpu.make_async_copy(scaled_one, scaled_one_out, store_sem.at[2]),
+    ]
+    for item in stores:
+        item.start()
+    tiles = copies.shape[2] // TILE
+    channels = cols.shape[1]
+
+    def raised_store(j, slot):
+        return pltpu.make_async_copy(tile.at[slot], raised_out.at[:, :, rows_of(j * TILE, TILE)], tile_sem.at[0, slot])
+
+    @pl.loop(0, tiles)
     def _(j):
         here = rows_of(j * TILE, TILE)
+        slot = j % 2
+
+        @pl.when(j >= 2)
+        def _():
+            raised_store(j - 2, slot).wait()
+
         for phase, (row_phase, col_phase) in enumerate(phase_pairs):
-            total = None
+            summed = None
             for k, r in phase_taps[row_phase]:
                 for l, q in phase_taps[col_phase]:
                     term = dot(full1[3 * k + l], copies[2 * r + q, :, here])
-                    total = term if total is None else total + term
-            raised[phase, :, here] = total
+                    summed = term if summed is None else summed + term
+            tile[slot, phase] = summed
             noise_row = gains[0] * noise[phase : phase + 1, here]
-            for i in range(raised.shape[1] // ROWS):
+            for i in range(channels // ROWS):
                 rows = slice(i * ROWS, (i + 1) * ROWS)
-                pre = raised[phase, rows, here] * wide(demod1[rows, :]) + noise_row + wide(cols[3, rows, :])
+                pre = tile[slot, phase, rows, :] * wide(demod1[rows, :]) + noise_row + wide(cols[3, rows, :])
                 act = pre * (0.6 * root_two + 0.4 * root_two * jnp.tanh(0.5 * pre))
                 scaled[phase, rows, here] = (act * wide(cols[1, rows, :])).astype(BF)
+
+        raised_store(j, slot).start()
 
         @pl.when(j == 1)
         def _():
@@ -549,16 +615,11 @@
                 near[1][k].wait_recv()
                 relay[1][k].start()
                 swap[1][k].start()
-            for item in grad_moves:
-                item.start()
+            for part in range(4):
+                for k in (1, 2, 3):
+                    grad_move(part, k).start()
             local3.start()
 
-    stores = [
-        pltpu.make_async_copy(raised, raised_out, store_sem.at[1]),
-        pltpu.make_async_copy(scaled, scaled_out, store_sem.at[2]),
-    ]
-    for item in stores:
-        item.start()
     make_copies(scaled, copies)
     for item in relay[1]:
         item.wait_recv()
@@ -566,8 +627,6 @@
     loads[3].wait()
     for item in swap[1]:
         item.wait_recv()
-    store2 = pltpu.make_async_copy(full2, full2_out, store_sem.at[3])
-    store2.start()
     demodulate(full2, rows_ref[4:5, :] * rows_ref[4:5, :], demod2)
     rgb_rows = jnp.concatenate([rows_ref[...] * rows_ref[5:6, :]] * 2, axis=0).astype(BF)
     live = gains[2]
@@ -575,11 +634,16 @@
 
     def tile_stores(j, slot):
         return (
-            pltpu.make_async_copy(conv_tile.at[slot], conv_out.at[:, :, rows_of(j * TILE, TILE)], tile_sem.at[0, slot]),
-            pltpu.make_async_copy(feat_tile.at[slot], feat_out.at[:, rows_of(j * 4 * TILE, 4 * TILE)], tile_sem.at[1, slot]),
+            pltpu.make_async_copy(tile.at[slot], conv_out.at[:, :, rows_of(j * TILE, TILE)], tile_sem.at[0, slot]),
+            pltpu.make_async_copy(grad_tile.at[slot], feat_natural.at[:, part_of(j)], tile_sem.at[1, slot]),
         )
 
-    @pl.loop(0, raised.shape[2] // TILE)
+    raised_store(2, 0).wait()
+    raised_store(3, 1).wait()
+    for item in stores:
+        item.wait()
+
+    @pl.loop(0, tiles)
     def _(j):
         here = rows_of(j * TILE, TILE)
         slot = j % 2
@@ -590,22 +654,25 @@
                 item.wait()
 
         for phase in range(4):
-            total = None
+            summed = None
             for t in range(9):
                 term = dot(full2[t], copies[copy_index(phase, t // 3 - 1, t % 3 - 1), :, here])
-                total = term if total is None else total + term
-            conv_tile[slot, phase] = total
+                summed = term if summed is None else summed + term
+            tile[slot, phase] = summed
             noise_row = gains[1] * noise[4 + phase : 5 + phase, here]
-            for i in range(raised.shape[1] // ROWS):
+            for i in range(channels // ROWS):
                 rows = slice(i * ROWS, (i + 1) * ROWS)
-                pre = conv_tile[slot, phase, rows, :] * wide(demod2[rows, :]) + noise_row + wide(cols[4, rows, :])
+                pre = tile[slot, phase, rows, :] * wide(demod2[rows, :]) + noise_row + wide(cols[4, rows, :])
                 act = pre * (0.6 * root_two + 0.4 * root_two * jnp.tanh(0.5 * pre))
                 out = (act * live).astype(BF)
+                low = slice(i * ROWS % 256, i * ROWS % 256 + ROWS)
                 for half in range(TILE // 128):
-                    ordered[half, rows, phase * 128 : (phase + 1) * 128] = out[:, half * 128 : (half + 1) * 128]
+                    core1[2 * half + i * ROWS // 256, low, phase * 128 : (phase + 1) * 128] = (
+                        out[:, half * 128 : (half + 1) * 128]
+                    )
         for half in range(TILE // 128):
-            image = dot(ordered[half], order[...]).astype(BF)
-            feat_tile[slot, :, half * 512 : (half + 1) * 512] = image
+            image = dot(core1[2 * half : 2 * half + 2].reshape(channels, 512), order[...]).astype(BF)
+            grad_tile[slot, :, half * 512 : (half + 1) * 512] = image
             pixels = rows_of(j * 4 * TILE + half * 512, 512)
             color[:, pixels] = dot(rgb_rows, image)
             rgb_grad[...] += dot_nt(stacked[:, pixels], image)
@@ -615,41 +682,9 @@
     for j in (2, 3):
         for item in tile_stores(j, j % 2):
             item.wait()
-    for item in [store1, store2, local3] + stores:
-        item.wait()
+    store1.wait()
     for item in pack_moves + x_moves + near[0] + near[1] + relay[0] + relay[1] + swap[0] + swap[1]:
         item.wait_send()
-    for item in grad_moves:
-        item.wait()
-
-
-def backward_kernel(gains, arrived, convolved, raised, scaled_two, full1, full2, feat_natural,
-                    scaled_one, x_all, cols, rows_ref, demod1, demod2, noise, order, color_phases, rgb_grad,
-                    style_weight, shared, color,
-                    feat_all, back_all, grad1_out, grad2_out, every, every_shared, latent_grad, color_in,
-                    sums2, sums1, sums0, inner2, inner1, style_sums, vectors, owned, latent_in, tile, grad_tile, copies, field, weight, total, back,
-                    keep, send, core1, core2, quad1, quad2, zsum1, zsum2, zin1, zin2, out1, out2,
-                    load_sem, tile_sem, feat_send, feat_recv, back_send, back_recv, core_send, core_recv,
-                    quad_send, quad_recv, z_send, z_recv, all_send, all_recv, twin_send, twin_recv,
-                    shared_send, shared_recv, every_send, every_recv, owned_send, owned_recv, latent_send, latent_recv, color_send, color_recv):
-    me = lax.axis_index("chan")
-    row = lax.axis_index("dp")
-    core = row % 2
-    depth = row // 2
-    twin = row + 1 - 2 * core
-    mesh_id = pl.DeviceIdType.MESH
-    chans = [me] + [chan_peer(me, k) for k in (1, 2, 3)]
-    depths = [depth] + [chan_peer(depth, k) for k in (1, 2, 3)]
-    barrier = pltpu.get_barrier_semaphore()
-    for k in (1, 2, 3):
-        pl.semaphore_signal(barrier, inc=1, device_id={"chan": chans[k]}, device_id_type=mesh_id)
-    lines = [depths[k] * 2 + core for k in (1, 2, 3)] + [twin] + [depths[k] * 2 + 1 - core for k in (1, 2, 3)]
-    for line in lines:
-        pl.semaphore_signal(barrier, inc=1, device_id={"dp": line}, device_id_type=mesh_id)
-    pl.semaphore_wait(barrier, 10)
-
-    def remote(source, target, sent, received, where):
-        return pltpu.make_async_remote_copy(source, target, sent, received, device_id=where, device_id_type=mesh_id)
 
     shared_moves = [
         remote(shared, every_shared.at[row], shared_send.at[i], shared_recv.at[i], {"dp": line})
@@ -671,32 +706,34 @@
     color_own.start()
 
     feat_moves = [
-        remote(feat_natural.at[rows_of(chans[k] * 128, 128), :], feat_all.at[me],
+        remote(feat_natural.at[rows_of(chans[k] * 128, 128), :], feat_all.at[rows_of(me * 128, 128), :],
                feat_send.at[k - 1], feat_recv.at[k - 1], {"chan": chans[k]})
         for k in (1, 2, 3)
     ]
     for item in feat_moves:
         item.start()
-    feat_own = pltpu.make_async_copy(feat_natural.at[rows_of(me * 128, 128), :], feat_all.at[me], load_sem.at[0])
+    feat_own = pltpu.make_async_copy(
+        feat_natural.at[rows_of(me * 128, 128), :], feat_all.at[rows_of(me * 128, 128), :], load_sem.at[0]
+    )
     feat_own.start()
-    load2 = pltpu.make_async_copy(full2, weight, load_sem.at[1])
-    load2.start()
-    load_field = pltpu.make_async_copy(scaled_two, field, load_sem.at[2])
-    load_field.start()
+    weight, keep, send = full2, full1.at[:, 0:256, :], full1.at[:, 256:512, :]
 
     def tiles_in(source, j, slot):
         return pltpu.make_async_copy(source.at[:, :, rows_of(j * TILE, TILE)], tile.at[slot], tile_sem.at[0, slot])
 
     def grads_in(j, slot):
         return pltpu.make_async_copy(
-            arrived.at[:, rows_of(j * 4 * TILE, 4 * TILE)], grad_tile.at[slot], tile_sem.at[1, slot]
+            arrived.at[:, part_of(j)], grad_tile.at[slot], tile_sem.at[1, slot]
         )
 
-    tiles_in(convolved, 0, 0).start()
-    grads_in(0, 0).start()
-    live = gains[2]
-    channels = cols.shape[1]
-    tiles = copies.shape[2] // TILE
+    def grads_ready(j):
+        for k in (1, 2, 3):
+            grad_move(j, k).wait_recv()
+        grads_in(j, j % 2).start()
+
+    tiles_in(conv_out, 0, 0).start()
+    local3.wait()
+    grads_ready(0)
     sums2[...] = jnp.zeros_like(sums2)
     sums1[...] = jnp.zeros_like(sums1)
     style_sums[...] = jnp.zeros_like(style_sums)
@@ -713,14 +750,14 @@
 
         @pl.when(j + 1 < tiles)
         def _():
-            tiles_in(convolved, j + 1, 1 - slot).start()
-            grads_in(j + 1, 1 - slot).start()
-
-        tiles_in(convolved, j, slot).wait()
+            tiles_in(conv_out, j + 1, 1 - slot).start()
+            grads_ready(j + 1)
+
+        tiles_in(conv_out, j, slot).wait()
         grads_in(j, slot).wait()
         here = rows_of(j * TILE, TILE)
         for half in range(TILE // 128):
-            total[half] = dot(grad_tile[slot, :, half * 512 : (half + 1) * 512], order[...])
+            total[half] = dot(grad_tile[slot, :, half * 512 : (half + 1) * 512], order_back[...])
         for phase in range(4):
             noise_plain = noise[4 + phase : 5 + phase, here]
             noise_row = gains[1] * noise_plain
@@ -741,10 +778,10 @@
                 copies[4 * phase, rows, here] = (grad * scale).astype(BF)
                 add_sums(sums2, rows, (grad * conv, grad, grad * noise_plain))
 
-    tiles_in(raised, 0, 0).start()
+    tiles_in(raised_out, 0, 0).start()
     late = [
-        pltpu.make_async_copy(scaled_one, grad_tile.at[0], load_sem.at[4]),
-        pltpu.make_async_copy(x_all, grad_tile.at[1], load_sem.at[5]),
+        pltpu.make_async_copy(scaled_one_out, grad_tile.at[0], load_sem.at[4]),
+        pltpu.make_async_copy(x_out, grad_tile.at[1], load_sem.at[5]),
     ]
     for item in late:
         item.start()
@@ -769,8 +806,6 @@
                     copies[4 * phase + 2 * r + q, rows, :] = move(value, row_sign * r, col_sign * q)
 
     spread_copies()
-    load2.wait()
-    load_field.wait()
 
     def split(c, slot, t, inner, square_row):
         for k in range(4):
@@ -780,11 +815,16 @@
                 column = jnp.concatenate([inner[rows, :]] * 4, axis=1)
                 plain = weight[t, rows, :].astype(F32)
                 scaled = plain * column
-                out[t, k] = (total[slot, rows, :] + scaled * square_row).astype(BF)
+                value = (total[slot, rows, :] + scaled * square_row).astype(BF)
+                out[t, k * 32 : (k + 1) * 32, :] = value[:32]
+                out[t, 128 + k * 32 : 160 + k * 32, :] = value[32:]
                 scaled = plain * scaled
                 style_sums[c] += sum(scaled[i * 8 : (i + 1) * 8, :] for i in range(8))
 
     cores, quads, zsums, zins, outs = (core1, core2), (quad1, quad2), (zsum1, zsum2), (zin1, zin2), (out1, out2)
+    firsts = (first1, first2)
+    low, high = depth % 2, depth // 2
+    beside, across = {"dp": depths[1] * 2 + core}, {"dp": depths[2] * 2 + core}
 
     def taps(g):
         return pl.ds(3 * g, 3)
@@ -792,17 +832,25 @@
     def core_move(c, g):
         return remote(send.at[taps(g)], cores[c].at[taps(g)], core_send.at[c, g], core_recv.at[c, g], {"dp": twin})
 
+    def first_move(c, g):
+        return remote(keep.at[taps(g), rows_of(128 - low * 128, 128), :], firsts[c].at[taps(g)],
+                      first_send.at[c, g], first_recv.at[c, g], beside)
+
     def quad_move(c, g, k):
-        return remote(keep.at[taps(g), k], quads[c].at[taps(g), k - 1], quad_send.at[c, g, k - 1],
-                      quad_recv.at[c, g, k - 1], {"chan": chans[k]})
-
-    def z_move(c, g, k):
-        return remote(zsums[c].at[taps(g), rows_of(depths[k] * 16, 16), :], zins[c].at[taps(g), k - 1],
-                      z_send.at[c, g, k - 1], z_recv.at[c, g, k - 1], {"dp": depths[k] * 2 + core})
-
-    def all_move(c, g, k):
-        part = outs[c].at[taps(g), rows_of(core * 64 + depth * 16, 16), :]
-        return remote(part, part, all_send.at[c, g, k - 1], all_recv.at[c, g, k - 1], {"dp": depths[k] * 2 + core})
+        return remote(keep.at[taps(g), rows_of(low * 128 + k * 32, 32), :], quads[c].at[taps(g), k - 1],
+                      quad_send.at[c, g, k - 1], quad_recv.at[c, g, k - 1], {"chan": chans[k]})
+
+    def z_move(c, g):
+        return remote(zsums[c].at[taps(g), rows_of(16 - high * 16, 16), :], zins[c].at[taps(g)],
+                      z_send.at[c, g], z_recv.at[c, g], across)
+
+    def across_move(c, g):
+        part = outs[c].at[taps(g), rows_of(core * 64 + low * 32 + high * 16, 16), :]
+        return remote(part, part, across_send.at[c, g], across_recv.at[c, g], across)
+
+    def beside_move(c, g):
+        part = outs[c].at[taps(g), rows_of(core * 64 + low * 32, 32), :]
+        return remote(part, part, beside_send.at[c, g], beside_recv.at[c, g], beside)
 
     def twin_move(c, g):
         part = outs[c].at[taps(g), rows_of(core * 64, 64), :]
@@ -812,8 +860,15 @@
         core_move(c, g).wait_recv()
         for i in range(3):
             t = 3 * g + i
-            for k in range(4):
-                keep[t, k] = (keep[t, k].astype(F32) + cores[c][t, k].astype(F32)).astype(BF)
+            keep[t] = (keep[t].astype(F32) + cores[c][t].astype(F32)).astype(BF)
+        first_move(c, g).start()
+
+    def join_first(c, g):
+        first_move(c, g).wait_recv()
+        rows = rows_of(low * 128, 128)
+        for i in range(3):
+            t = 3 * g + i
+            keep[t, rows, :] = (keep[t, rows, :].astype(F32) + firsts[c][t].astype(F32)).astype(BF)
         for k in (1, 2, 3):
             quad_move(c, g, k).start()
 
@@ -822,28 +877,26 @@
             quad_move(c, g, k).wait_recv()
         for i in range(3):
             t = 3 * g + i
-            value = keep[t, 0].astype(F32)
+            value = keep[t, rows_of(low * 128, 32), :].astype(F32)
             for k in range(3):
                 value = value + quads[c][t, k].astype(F32)
             zsums[c][t] = value.astype(BF)
-        for k in (1, 2, 3):
-            z_move(c, g, k).start()
+        z_move(c, g).start()
 
     def join_depth(c, g):
-        for k in (1, 2, 3):
-            z_move(c, g, k).wait_recv()
+        z_move(c, g).wait_recv()
         for i in range(3):
             t = 3 * g + i
-            value = zsums[c][t, rows_of(depth * 16, 16), :].astype(F32)
-            for k in range(3):
-                value = value + zins[c][t, k].astype(F32)
-            outs[c][t, rows_of(core * 64 + depth * 16, 16), :] = value.astype(BF)
-        for k in (1, 2, 3):
-            all_move(c, g, k).start()
-
-    def join_all(c, g):
-        for k in (1, 2, 3):
-            all_move(c, g, k).wait_recv()
+            value = zsums[c][t, rows_of(high * 16, 16), :].astype(F32) + zins[c][t].astype(F32)
+            outs[c][t, rows_of(core * 64 + low * 32 + high * 16, 16), :] = value.astype(BF)
+        across_move(c, g).start()
+
+    def join_across(c, g):
+        across_move(c, g).wait_recv()
+        beside_move(c, g).start()
+
+    def join_beside(c, g):
+        beside_move(c, g).wait_recv()
         twin_move(c, g).start()
 
     def weight_grad(c, product, inner, square_row):
@@ -893,9 +946,9 @@
 
         @pl.when(j + 1 < tiles)
         def _():
-            tiles_in(raised, j + 1, 1 - slot).start()
-
-        tiles_in(raised, j, slot).wait()
+            tiles_in(raised_out, j + 1, 1 - slot).start()
+
+        tiles_in(raised_out, j, slot).wait()
         here = rows_of(j * TILE, TILE)
         for phase in range(4):
             summed = None
@@ -918,13 +971,22 @@
                 field[phase, rows, here] = (grad * scale).astype(BF)
                 add_sums(sums1, rows, (grad * conv, grad, grad * noise_plain, value * act))
 
+        @pl.when(j == 0)
+        def _():
+            join_first(1, 0)
+            join_first(1, 1)
+
+        @pl.when(j == 1)
+        def _():
+            join_first(1, 2)
+
         @pl.when(j == 2)
         def _():
             join_quad(1, 0)
             join_quad(1, 1)
 
     inner_of(sums1, demod1, inner1)
-    load1 = pltpu.make_async_copy(full1, weight, load_sem.at[1])
+    load1 = pltpu.make_async_copy(full1_out, weight, load_sem.at[1])
     load1.start()
 
     @pl.loop(0, channels // 32)
@@ -940,6 +1002,7 @@
     for g in range(3):
         for k in (1, 2, 3):
             quad_move(1, g, k).wait_send()
+        first_move(1, g).wait_send()
     load1.wait()
     for item in late:
         item.wait()
@@ -969,7 +1032,9 @@
             item = item[:, :128] + item[:, 128:]
             sums0[rows, :] = item if n == 0 else sums0[rows, :] + item
         if n == 1:
-            join_quad(0, 0)
+            join_first(0, 0)
+        if n == 3:
+            join_first(0, 1)
     back_moves = [
         remote(copies.at[9, rows_of(chans[k] * 128, 128), :], back_all.at[me],
                back_send.at[k - 1], back_recv.at[k - 1], {"chan": chans[k]})
@@ -1010,9 +1075,9 @@
     owned[me] = vectors[me]
 
     for g in range(3):
-        join_all(1, g)
-    join_quad(0, 1)
-    join_depth(0, 0)
+        join_across(1, g)
+    join_quad(0, 0)
+    join_first(0, 2)
     for item in owned_moves:
         item.wait_recv()
     for item in style_loads:
@@ -1036,35 +1101,90 @@
     for item in latent_moves + every_moves:
         item.start()
     every[row] = owned[...]
-    join_quad(0, 2)
-    join_depth(0, 1)
-    join_all(0, 0)
+    join_depth(0, 0)
+    join_quad(0, 1)
+    for g in range(3):
+        join_beside(1, g)
+
+    for item in feat_moves:
+        item.wait_recv()
+    feat_own.wait()
+
+    def feat_in(n, half):
+        return pltpu.make_async_copy(
+            feat_all.at[half * 256 : (half + 1) * 256, n * 512 : (n + 1) * 512], core2.at[n % 4 * 2 + half],
+            image_sem.at[n % 4, half],
+        )
+
+    def feat_store(n):
+        return pltpu.make_async_copy(
+            raw.at[n % 2], feat_out.at[:, :, n * 512 : (n + 1) * 512], raw_sem.at[n % 2]
+        )
+
+    for n in range(4):
+        feat_in(n, 0).start()
+        feat_in(n, 1).start()
+    for n in range(8):
+        if n >= 2:
+            feat_store(n - 2).wait()
+        feat_in(n, 0).wait()
+        feat_in(n, 1).wait()
+
+        @pl.loop(0, 8)
+        def _(i):
+            value = jnp.stack(
+                [core2[n % 4 * 2 + image // 2, rows_of(image % 2 * 128 + i * 16, 16), :] for image in range(4)]
+            )
+            raw[n % 2, rows_of(i * 16, 16), :, :] = jnp.swapaxes(value, 0, 1)
+
+        feat_store(n).start()
+        if n + 4 < 8:
+            feat_in(n + 4, 0).start()
+            feat_in(n + 4, 1).start()
+        if n == 2:
+            join_depth(0, 1)
+        if n == 4:
+            join_across(0, 0)
+            join_quad(0, 2)
+        if n == 6:
+            join_across(0, 1)
+            join_beside(0, 0)
     join_depth(0, 2)
-    join_all(0, 1)
+    join_beside(0, 1)
     for g in range(3):
         twin_move(1, g).wait()
     store2 = pltpu.make_async_copy(out2, grad2_out, load_sem.at[1])
     store2.start()
-    join_all(0, 2)
+    join_across(0, 2)
     for item in latent_moves:
         item.wait_recv()
     latent_grad[...] = latent_in[0] + latent_in[1] + latent_in[2] + latent_in[3]
+    join_beside(0, 2)
     for g in range(3):
         twin_move(0, g).wait()
     store1 = pltpu.make_async_copy(out1, grad1_out, load_sem.at[3])
     store1.start()
+    feat_store(6).wait()
+    feat_store(7).wait()
     for c in (0, 1):
         for g in range(3):
-            for k in (1, 2, 3):
-                if c == 0:
+            if c == 0:
+                first_move(c, g).wait_send()
+                for k in (1, 2, 3):
                     quad_move(c, g, k).wait_send()
-                z_move(c, g, k).wait_send()
-                all_move(c, g, k).wait_send()
-    for item in feat_moves + back_moves + shared_moves + every_moves + color_moves:
+            z_move(c, g).wait_send()
+            across_move(c, g).wait_send()
+            beside_move(c, g).wait_send()
+    for item in feat_moves:
+        item.wait_send()
+    for item in back_moves + shared_moves + every_moves + color_moves:
         item.wait()
     for item in owned_moves + latent_moves:
         item.wait_send()
-    for item in (feat_own, back_own, color_own, store2, store1):
+    for j in range(4):
+        for k in (1, 2, 3):
+            grad_move(j, k).wait_send()
+    for item in (back_own, color_own, store2, store1):
         item.wait()
 
 
@@ -1115,95 +1235,48 @@
          jnp.zeros((3, pixels), F32)]
     )
     x_by_image = feat_in.transpose(1, 0, 2)
-    grad_by_image = feat_grad.transpose(1, 0, 2)
     order = phase_order()
 
     vmem = pl.BlockSpec(memory_space=pltpu.VMEM)
     field, wide_weight = (4, channels, half_pix), (9, channels, channels)
-    vector = ((channels, 128), F32)
-    forward_outs = (
-        (field, F32), (field, BF), (field, F32), ((channels, pixels), BF), (wide_weight, BF), (wide_weight, BF),
-        ((channels, pixels), BF), ((channels, half_pix), BF), ((channels, half_pix), BF), vector, vector,
-        ((16, pixels), F32), ((16, channels), F32), ((5, channels, 128), F32), ((8, channels), F32),
-        ((8, half_pix), F32), ((4, 16, half_pix), BF),
-    )
-    (raised, scaled_two, convolved, feat_natural, full_one, full_two, grad_arrived,
-     x_all, scaled_one, demod_one, demod_two, color, rgb_part, cols, row_vectors, noise, color_phases) = pl.pallas_call(
-        forward_kernel,
-        in_specs=[SMEM, ANY, ANY, ANY, ANY, ANY, vmem, vmem, vmem],
-        out_specs=[ANY] * 7 + [vmem] * 10,
-        out_shape=[jax.ShapeDtypeStruct(shape, dtype) for shape, dtype in forward_outs],
-        scratch_shapes=[
-            pltpu.VMEM(field, F32),
-            pltpu.VMEM(field, BF),
-            pltpu.VMEM(wide_weight, BF),
-            pltpu.VMEM(wide_weight, BF),
-            pltpu.VMEM((16, channels, half_pix), BF),
-            pltpu.VMEM((2, 4, channels, TILE), F32),
-            pltpu.VMEM((2, channels, 4 * TILE), BF),
-            pltpu.VMEM((TILE // 128, channels, 512), BF),
-            pltpu.VMEM((4, 8, 128), F32),
-            pltpu.VMEM((16, pixels), BF),
-            pltpu.SemaphoreType.DMA((4,)),
-            pltpu.SemaphoreType.DMA((5,)),
-            pltpu.SemaphoreType.DMA((2, 2)),
-        ]
-        + [pltpu.SemaphoreType.DMA((3,))] * 4
-        + [pltpu.SemaphoreType.DMA((2, 4))] * 2
-        + [pltpu.SemaphoreType.DMA((2, 3))] * 2
-        + [pltpu.SemaphoreType.DMA((3,))] * 2,
-        compiler_params=pltpu.CompilerParams(vmem_limit_bytes=LIMIT, collective_id=0, has_side_effects=True),
-        cost_estimate=pl.CostEstimate(flops=int(50e9), bytes_accessed=12 << 20, transcendentals=0),
-    )(gains, pack, x_by_image, conv_first, conv_second, grad_by_image, plain, order.T, order)
-
     rgb_cot = rgb_grad * live_mask[:, None, None]
     rgb_bias_part = jnp.sum(rgb_cot, axis=(0, 2))
     shared = jnp.concatenate([latent, jnp.broadcast_to(jnp.pad(rgb_bias_part, (0, 509))[None], (4, 512))])
-    backward_outs = (
-        ((4, local_ch, pixels), BF), ((4, local_ch, half_pix), BF), ((9, local_ch, channels), BF),
-        ((9, local_ch, channels), BF), ((8, 4, 16, 128), F32), ((8, 8, 512), F32), ((8, 512), F32),
-        ((4, 8, pixels // 4), F32),
-    )
-    feat_all, back_all, grad_one, grad_two, every, every_shared, latent_grad, color_in = pl.pallas_call(
-        backward_kernel,
-        in_specs=[SMEM] + [ANY] * 9 + [vmem] * 8 + [ANY, vmem, ANY],
-        out_specs=[ANY] * 4 + [vmem] * 3 + [ANY],
-        out_shape=[jax.ShapeDtypeStruct(shape, dtype) for shape, dtype in backward_outs],
-        scratch_shapes=[
-            pltpu.VMEM((3, channels, 128), F32),
-            pltpu.VMEM((4, channels, 128), F32),
-            pltpu.VMEM((channels, 128), F32),
-            pltpu.VMEM((channels, 128), F32),
-            pltpu.VMEM((channels, 128), F32),
-            pltpu.VMEM((2, 8, channels), F32),
-            pltpu.VMEM((4, 16, 128), F32),
-            pltpu.VMEM((4, 16, 128), F32),
-            pltpu.VMEM((4, 8, 512), F32),
-            pltpu.VMEM((2, 4, channels, TILE), F32),
-            pltpu.VMEM((2, channels, 4 * TILE), BF),
-            pltpu.VMEM((16, channels, half_pix), BF),
-            pltpu.VMEM(field, BF),
-            pltpu.VMEM(wide_weight, BF),
-            pltpu.VMEM((2, channels, channels), F32),
-            pltpu.VMEM((2, channels, TILE), F32),
-        ]
-        + [pltpu.VMEM((9, 4, 64, channels), BF)] * 4
-        + [pltpu.VMEM((9, 3, 64, channels), BF)] * 2
-        + [pltpu.VMEM((9, 64, channels), BF)] * 2
-        + [pltpu.VMEM((9, 3, 16, channels), BF)] * 2
-        + [pltpu.VMEM((9, local_ch, channels), BF)] * 2
-        + [pltpu.SemaphoreType.DMA((10,)), pltpu.SemaphoreType.DMA((2, 2))]
-        + [pltpu.SemaphoreType.DMA((3,))] * 4
-        + [pltpu.SemaphoreType.DMA((2, 3))] * 2
-        + [pltpu.SemaphoreType.DMA((2, 3, 3))] * 6
-        + [pltpu.SemaphoreType.DMA((2, 3))] * 2
-        + [pltpu.SemaphoreType.DMA((7,))] * 4
-        + [pltpu.SemaphoreType.DMA((3,))] * 6,
-        compiler_params=pltpu.CompilerParams(vmem_limit_bytes=LIMIT, collective_id=1, has_side_effects=True),
-        cost_estimate=pl.CostEstimate(flops=int(100e9), bytes_accessed=12 << 20, transcendentals=0),
-    )(gains, grad_arrived, convolved, raised, scaled_two, full_one, full_two, feat_natural, scaled_one, x_all,
-      cols, row_vectors, demod_one, demod_two, noise, order.T, color_phases, rgb_part, style_weight, shared, color)
-    feat_out = feat_all.transpose(1, 0, 2)
+    outs = (
+        (field, F32), (field, F32), ((channels, pixels), BF), (wide_weight, BF), ((channels, pixels), BF),
+        ((channels, half_pix), BF), ((channels, half_pix), BF), ((channels, pixels), BF), ((channels, pixels), BF),
+        (feat_grad.shape, BF), ((4, local_ch, half_pix), BF), ((9, local_ch, channels), BF),
+        ((9, local_ch, channels), BF), ((4, 8, pixels // 4), F32), ((8, 4, 16, 128), F32), ((8, 8, 512), F32),
+        ((8, 512), F32),
+    )
+    vector = ((channels, 128), F32)
+    scratch = (
+        vector, vector, ((16, pixels), F32), ((16, channels), F32), ((5, channels, 128), F32), ((8, channels), F32),
+        ((8, half_pix), F32), ((4, 16, half_pix), BF), ((4, 8, 128), F32), ((16, pixels), BF),
+        (wide_weight, BF), (wide_weight, BF), ((16, channels, half_pix), BF), ((2, 4, channels, TILE), F32),
+        ((2, channels, 4 * TILE), BF), (field, BF), ((2, channels, channels), F32), ((2, channels, TILE), F32),
+        ((9, 256, channels), BF), ((9, 256, channels), BF), ((9, 128, channels), BF), ((9, 128, channels), BF),
+        ((9, 3, 32, channels), BF), ((9, 3, 32, channels), BF), ((9, 32, channels), BF), ((9, 32, channels), BF),
+        ((9, 16, channels), BF), ((9, 16, channels), BF),
+        ((9, local_ch, channels), BF), ((9, local_ch, channels), BF),
+        ((3, channels, 128), F32), ((4, channels, 128), F32), vector, vector, vector, ((2, 8, channels), F32),
+        ((4, 16, 128), F32), ((4, 16, 128), F32), ((4, 8, 512), F32), ((2, local_ch, 4, 512), BF),
+    )
+    counts = (
+        [(10,), (5,), (2, 2)] + [(3,)] * 4 + [(2, 4)] * 2 + [(2, 3)] * 2 + [(4, 3)] * 2 + [(3,)] * 4
+        + [(2, 3)] * 2 + [(2, 3, 3)] * 2 + [(2, 3)] * 10 + [(7,)] * 4 + [(3,)] * 6 + [(2,), (4, 2)]
+    )
+    results = pl.pallas_call(
+        block_kernel,
+        in_specs=[SMEM] + [ANY] * 5 + [vmem] * 3 + [ANY, vmem],
+        out_specs=[ANY] * 14 + [vmem] * 3,
+        out_shape=[jax.ShapeDtypeStruct(shape, dtype) for shape, dtype in outs],
+        scratch_shapes=[pltpu.VMEM(shape, dtype) for shape, dtype in scratch]
+        + [pltpu.SemaphoreType.DMA(count) for count in counts],
+        compiler_params=pltpu.CompilerParams(vmem_limit_bytes=LIMIT, collective_id=0, has_side_effects=True),
+        cost_estimate=pl.CostEstimate(flops=int(150e9), bytes_accessed=12 << 20, transcendentals=0),
+    )(gains, pack, x_by_image, conv_first, conv_second, feat_grad, plain, order.T, order, style_weight, shared)
+    feat_out, back_all, grad_one, grad_two, color_in, every, every_shared, latent_grad = results[9:]
     feat_in_grad = back_all.transpose(1, 0, 2).astype(F32)
     grad_one, grad_two = grad_one.astype(F32), grad_two.astype(F32)
 

time: 308 us -> 290 us (0.942)
  local copies, waits for them, and re-layouts: 28.2 us -> 17.9 us
  Pallas kernels: 256 us -> 246 us
    unnamed x30 -> x23, local copies, waits for them, and re-layouts: 19.8 us -> 7.8 us
    pallas_call x2 -> x1, Pallas kernels: 256 us -> 246 us  [image_body(): pl.pallas_call(block_kernel, in_specs=[SMEM] + [ANY] * 5 + [vmem] * 3 + [...]
where the time goes in v1:
time: 290 us; the launch traced here: 285 us
  Pallas kernels  246 us (85%)
  local copies, waits for them, and re-layouts  17.9 us (6%)
  other arithmetic  14 us (5%)
  matrix products  5.31 us (2%)
    pallas_call x1, Pallas kernels, image_body(): pl.pallas_call(block_kernel, in_specs=[SMEM] + [ANY] * 5 + [vmem] * 3 + [...  246 us
    unnamed x23, local copies, waits for them, and re-layouts  7.8 us

profile of v1, /device:TPU:0, one launch (start us, length us, event | category | flops | bytes accessed | tf_op | source)
XLA Modules:
  0.0 285.0 jit_solution(10316621598868776373)
XLA Ops:
  1.4 1.2 pad_maximum_fusion.2.gains
  3.4 1.6 fusion.18
  7.1 0.9 constant_dynamic-slice_fusion.1
  8.0 1.0 constant_dynamic-slice_fusion.3
  9.0 0.7 maximum_maximum_fusion.plain
  9.7 0.9 reshape.186
  11.1 0.8 fusion.6
  12.8 1.1 fusion.74
  13.9 1.3 pad_maximum_fusion.1.shared
  16.1 0.8 reshape.189
  16.9 1.1 fusion.1
  18.0 1.3 copy.81
  19.3 245.8 %shard_map.255 = (f32[4,512,1024]{2,1,0:T(8,128)}, f32[4,512,1024]{2,1,0:T(8,128)}, bf16[512,4096]{1,0:T(8,128)(2,1)}, bf16[9,512,512]{2,1,0:T(8,128)(2,1)}, bf1...) custom-call(f32[3]{0:T(128)} %pad_maximum_fusion.2.gains, ...), custom_call_target="tpu_custom_call" | custom-call | flops 149999992832 | bytes 12582912 | tf_op jit(solution)/shard_map/pallas_call | solution.py:1269
  265.2 1.4 slice_reduce_fusion
  266.6 1.0 reduce_sum.28
  267.6 0.9 slice.29
  270.2 1.3 slice.28
  271.6 1.0 fusion.9
  273.2 1.7 convolution_bitcast_fusion
  275.0 1.1 copy.48
  276.4 2.7 copy.47
  279.1 1.7 convert_element_type.39
  280.8 1.7 convert_element_type.40
  282.5 2.0 copy.84
  (41 shorter events, 7.8 us)
Async XLA Ops:
  0.6 17.4 %copy-start.4 = (bf16[128,4,1024]{2,1,0:T(4,128)(2,1)S(1)}, bf16[128,4,1024]{2,1,0:T(4,128)(2,1)}, u32[]{:S(2)}) copy-start(bf16[128,4,1024]{2,1,0:T(4,128)(2,1)} %param.16) | copy-start | bytes 3145732
  1.4 17.9 %copy-start.6 = (f32[4]{0:T(128)}, f32[4]{0:T(128)S(1)}, u32[]{:S(2)}) copy-start(f32[4]{0:T(128)S(1)} %compare_convert_fusion) | copy-start | bytes 52
  19.3 252.2 %copy-start.5 = (f32[4,3,1024]{2,0,1:T(4,128)S(1)}, f32[4,3,1024]{2,0,1:T(4,128)}, u32[]{:S(2)}) copy-start(f32[4,3,1024]{2,0,1:T(4,128)} %constant_dynamic-slice_fusion) | copy-start | bytes 147460
  19.3 252.2 %copy-start.7 = (f32[4]{0:T(128)S(1)}, f32[4]{0:T(128)}, u32[]{:S(2)}) copy-start(f32[4]{0:T(128)} %copy-done.6) | copy-start | bytes 52
  19.3 252.2 %copy-start.8 = (f32[3]{0:T(128)S(1)}, f32[3]{0:T(128)}, u32[]{:S(2)}) copy-start(f32[3]{0:T(128)} %param.28) | copy-start | bytes 40
  265.2 11.0 %copy-start.3 = (bf16[4,128,1024]{2,1,0:T(8,128)(2,1)S(1)}, bf16[4,128,1024]{2,1,0:T(8,128)(2,1)}, u32[]{:S(2)}) copy-start(bf16[4,128,1024]{2,1,0:T(8,128)(2,1)} %get-tuple-element.23) | copy-start | bytes 3145732
  275.0 4.1 %copy-start.2 = (bf16[9,128,512]{2,1,0:T(8,128)(2,1)S(1)}, bf16[9,128,512]{2,1,0:T(8,128)(2,1)}, u32[]{:S(2)}) copy-start(bf16[9,128,512]{2,1,0:T(8,128)(2,1)} %get-tuple-element.25) | copy-start | bytes 3538948
  276.4 4.4 %copy-start.1 = (bf16[9,128,512]{2,1,0:T(8,128)(2,1)S(1)}, bf16[9,128,512]{2,1,0:T(8,128)(2,1)}, u32[]{:S(2)}) copy-start(bf16[9,128,512]{2,1,0:T(8,128)(2,1)} %get-tuple-element.26) | copy-start | bytes 3538948
  279.1 3.5 %copy-start = (bf16[128,4,4096]{2,1,0:T(4,128)(2,1)S(1)}, bf16[128,4,4096]{2,1,0:T(4,128)(2,1)}, u32[]{:S(2)}) copy-start(bf16[128,4,4096]{2,1,0:T(4,128)(2,1)} %get-tuple-element.78) | copy-start | bytes 12582916

commit v2 on v1

--- a/solution.py
+++ b/solution.py
@@ -327,12 +327,12 @@
     if offset == 0:
         return field
     cells = field.shape[1]
-    lane = lax.broadcasted_iota(jnp.int32, field.shape, 1)
+    lane = lax.broadcasted_iota(jnp.int32, (1, cells), 1)
     row, col = lane // HALF, lane % HALF
     inside = (row + row_shift >= 0) & (row + row_shift < HALF)
     inside = inside & (col + col_shift >= 0) & (col + col_shift < HALF)
-    rolled = pltpu.roll(field.astype(F32), (-offset) % cells, 1)
-    return jnp.where(inside, rolled, 0.0).astype(field.dtype)
+    rolled = pltpu.roll(field, (-offset) % cells, 1)
+    return rolled * jnp.where(inside, 1.0, 0.0).astype(field.dtype)
 
 
 def near(parity, step):
@@ -431,7 +431,7 @@
                  core_send, core_recv, quad_send, quad_recv, z_send, z_recv, across_send, across_recv, twin_send, twin_recv,
                  first_send, first_recv, beside_send, beside_recv,
                  shared_send, shared_recv, every_send, every_recv, owned_send, owned_recv, latent_send, latent_recv,
-                 color_send, color_recv, raw_sem, image_sem):
+                 color_send, color_recv, raw_sem, image_sem, side_send, side_recv):
     me = lax.axis_index("chan")
     row = lax.axis_index("dp")
     core = row % 2
@@ -461,30 +461,63 @@
                {"chan": chans[k]})
         for k in (1, 2, 3)
     ]
-    for item in pack_moves + x_moves:
+    for item in pack_moves:
         item.start()
 
-    def half_rows(k):
-        return rows_of(chans[k] * 128 + core * 64, 64)
+    low, high = depth % 2, depth // 2
+    beside, across = {"dp": depths[1] * 2 + core}, {"dp": depths[2] * 2 + core}
+
+    def piece(k):
+        return pl.ds(pl.multiple_of(chans[k] * 128 + core * 64 + low * 16, 16), 48)
+
+    def outer(k, which):
+        return rows_of(chans[k] * 128 + core * 64 + which * 48, 16)
 
     fulls, owns = (full1, full2), (own1, own2)
     cut = 5
 
     def near_move(c, k):
-        return remote(owns[c].at[:, rows_of(core * 64, 64), :], fulls[c].at[:, half_rows(0), :],
+        return remote(owns[c].at[:, pl.ds(pl.multiple_of(core * 64 + low * 16, 16), 48), :], fulls[c].at[:, piece(0), :],
                       w_send.at[c, k - 1], w_recv.at[c, k - 1], {"chan": chans[k]})
 
     def relay_move(c, k):
-        part = fulls[c].at[pl.ds(0, cut) if k == 1 else pl.ds(cut, 9 - cut), half_rows(k), :]
+        part = fulls[c].at[pl.ds(0, cut) if k == 1 else pl.ds(cut, 9 - cut), piece(k), :]
         return remote(part, part, w_send.at[c, 1 + k], w_recv.at[c, 1 + k], {"chan": chans[3 - k]})
 
-    def swap_move(c, k):
-        part = fulls[c].at[:, half_rows(k), :]
-        return remote(part, part, swap_send.at[c, k - 1], swap_recv.at[c, k - 1], {"dp": twin})
+    def side_move(c, k):
+        part = fulls[c].at[:, outer(k, low), :]
+        return remote(part, part, side_send.at[c, k - 1], side_recv.at[c, k - 1], beside)
+
+    def swap_move(c, k, far):
+        part = fulls[c].at[:, outer(k, 1 - low) if far else piece(k), :]
+        n = k - 1 + 3 * far
+        return remote(part, part, swap_send.at[c, n], swap_recv.at[c, n], {"dp": twin})
 
     near = [[near_move(c, k) for k in (1, 2)] for c in (0, 1)]
     relay = [[relay_move(c, k) for k in (1, 2)] for c in (0, 1)]
-    swap = [[swap_move(c, k) for k in (1, 2, 3)] for c in (0, 1)]
+    side = [[side_move(c, k) for k in (1, 2, 3)] for c in (0, 1)]
+    swap = [[swap_move(c, k, far) for far in (0, 1) for k in (1, 2, 3)] for c in (0, 1)]
+
+    def weights_near(c):
+        for k in (0, 1):
+            near[c][k].wait_recv()
+            relay[c][k].start()
+            side[c][k].start()
+            swap[c][k].start()
+
+    def weights_diagonal(c):
+        for item in relay[c]:
+            item.wait_recv()
+        side[c][2].start()
+        swap[c][2].start()
+
+    def weights_done(c):
+        for k in range(3):
+            side[c][k].wait_recv()
+            swap[c][3 + k].start()
+        loads[2 + c].wait()
+        for item in swap[c]:
+            item.wait_recv()
 
     for item in near[0]:
         item.start()
@@ -527,6 +560,14 @@
         image_store(n, 1).start()
         if n + 2 < 8:
             raw_in(n + 2).start()
+        if n == 1:
+            weights_near(0)
+            for item in x_moves:
+                item.start()
+        if n == 6:
+            weights_diagonal(0)
+            for item in near[1]:
+                item.start()
     loads[0].wait()
     for item in pack_moves:
         item.wait_recv()
@@ -545,18 +586,7 @@
             for q in (0, 1):
                 copies[2 * r + q, rows, :] = move(value, r, q)
 
-    for k in (0, 1):
-        near[0][k].wait_recv()
-        relay[0][k].start()
-        swap[0][k].start()
-    for item in near[1]:
-        item.start()
-    for item in relay[0]:
-        item.wait_recv()
-    swap[0][2].start()
-    loads[2].wait()
-    for item in swap[0]:
-        item.wait_recv()
+    weights_done(0)
     store1 = pltpu.make_async_copy(full1, full1_out, store_sem.at[0])
     store1.start()
     demodulate(full1, rows_ref[3:4, :] * rows_ref[3:4, :], demod1)
@@ -609,24 +639,20 @@
 
         raised_store(j, slot).start()
 
-        @pl.when(j == 1)
+        @pl.when(j == 0)
         def _():
-            for k in (0, 1):
-                near[1][k].wait_recv()
-                relay[1][k].start()
-                swap[1][k].start()
+            weights_near(1)
             for part in range(4):
                 for k in (1, 2, 3):
                     grad_move(part, k).start()
             local3.start()
 
+        @pl.when(j == 1)
+        def _():
+            weights_diagonal(1)
+
     make_copies(scaled, copies)
-    for item in relay[1]:
-        item.wait_recv()
-    swap[1][2].start()
-    loads[3].wait()
-    for item in swap[1]:
-        item.wait_recv()
+    weights_done(1)
     demodulate(full2, rows_ref[4:5, :] * rows_ref[4:5, :], demod2)
     rgb_rows = jnp.concatenate([rows_ref[...] * rows_ref[5:6, :]] * 2, axis=0).astype(BF)
     live = gains[2]
@@ -683,7 +709,7 @@
         for item in tile_stores(j, j % 2):
             item.wait()
     store1.wait()
-    for item in pack_moves + x_moves + near[0] + near[1] + relay[0] + relay[1] + swap[0] + swap[1]:
+    for item in pack_moves + x_moves + near[0] + near[1] + relay[0] + relay[1] + side[0] + side[1] + swap[0] + swap[1]:
         item.wait_send()
 
     shared_moves = [
@@ -823,8 +849,6 @@
 
     cores, quads, zsums, zins, outs = (core1, core2), (quad1, quad2), (zsum1, zsum2), (zin1, zin2), (out1, out2)
     firsts = (first1, first2)
-    low, high = depth % 2, depth // 2
-    beside, across = {"dp": depths[1] * 2 + core}, {"dp": depths[2] * 2 + core}
 
     def taps(g):
         return pl.ds(3 * g, 3)
@@ -974,15 +998,15 @@
         @pl.when(j == 0)
         def _():
             join_first(1, 0)
-            join_first(1, 1)
 
         @pl.when(j == 1)
         def _():
-            join_first(1, 2)
+            join_first(1, 1)
+            join_quad(1, 0)
 
         @pl.when(j == 2)
         def _():
-            join_quad(1, 0)
+            join_first(1, 2)
             join_quad(1, 1)
 
     inner_of(sums1, demod1, inner1)
@@ -1033,8 +1057,6 @@
             sums0[rows, :] = item if n == 0 else sums0[rows, :] + item
         if n == 1:
             join_first(0, 0)
-        if n == 3:
-            join_first(0, 1)
     back_moves = [
         remote(copies.at[9, rows_of(chans[k] * 128, 128), :], back_all.at[me],
                back_send.at[k - 1], back_recv.at[k - 1], {"chan": chans[k]})
@@ -1042,6 +1064,7 @@
     ]
     for item in back_moves:
         item.start()
+    join_first(0, 1)
     back_own = pltpu.make_async_copy(copies.at[9, rows_of(me * 128, 128), :], back_all.at[me], load_sem.at[2])
     back_own.start()
 
@@ -1263,8 +1286,8 @@
         ((4, 16, 128), F32), ((4, 16, 128), F32), ((4, 8, 512), F32), ((2, local_ch, 4, 512), BF),
     )
     counts = (
-        [(10,), (5,), (2, 2)] + [(3,)] * 4 + [(2, 4)] * 2 + [(2, 3)] * 2 + [(4, 3)] * 2 + [(3,)] * 4
-        + [(2, 3)] * 2 + [(2, 3, 3)] * 2 + [(2, 3)] * 10 + [(7,)] * 4 + [(3,)] * 6 + [(2,), (4, 2)]
+        [(10,), (5,), (2, 2)] + [(3,)] * 4 + [(2, 4)] * 2 + [(2, 6)] * 2 + [(4, 3)] * 2 + [(3,)] * 4
+        + [(2, 3)] * 2 + [(2, 3, 3)] * 2 + [(2, 3)] * 10 + [(7,)] * 4 + [(3,)] * 6 + [(2,), (4, 2), (2, 3), (2, 3)]
     )
     results = pl.pallas_call(
         block_kernel,

time: 290 us -> 276 us (0.952)
  Pallas kernels: 246 us -> 232 us
    pallas_call x1, Pallas kernels: 246 us -> 232 us  [image_body(): pl.pallas_call(block_kernel, in_specs=[SMEM] + [ANY] * 5 + [vmem] * 3 + [...]
where the time goes in v2:
time: 276 us; the launch traced here: 272 us
  Pallas kernels  232 us (84%)
  local copies, waits for them, and re-layouts  17.9 us (6%)
  other arithmetic  14 us (5%)
  matrix products  5.31 us (2%)
    pallas_call x1, Pallas kernels, image_body(): pl.pallas_call(block_kernel, in_specs=[SMEM] + [ANY] * 5 + [vmem] * 3 + [...  232 us
    unnamed x23, local copies, waits for them, and re-layouts  7.8 us

profile of v2, /device:TPU:0, one launch (start us, length us, event | category | flops | bytes accessed | tf_op | source)
XLA Modules:
  0.0 271.5 jit_solution(5427104851556557402)
XLA Ops:
  1.4 1.2 pad_maximum_fusion.2.gains
  3.4 1.6 fusion.18
  7.1 0.9 constant_dynamic-slice_fusion.1
  8.0 1.0 constant_dynamic-slice_fusion.3
  9.0 0.7 maximum_maximum_fusion.plain
  9.7 0.9 reshape.186
  11.1 0.8 fusion.6
  12.8 1.1 fusion.74
  13.9 1.3 pad_maximum_fusion.1.shared
  16.1 0.8 reshape.189
  16.9 1.1 fusion.1
  18.0 1.3 copy.81
  19.3 232.4 %shard_map.255 = (f32[4,512,1024]{2,1,0:T(8,128)}, f32[4,512,1024]{2,1,0:T(8,128)}, bf16[512,4096]{1,0:T(8,128)(2,1)}, bf16[9,512,512]{2,1,0:T(8,128)(2,1)}, bf1...) custom-call(f32[3]{0:T(128)} %pad_maximum_fusion.2.gains, ...), custom_call_target="tpu_custom_call" | custom-call | flops 149999992832 | bytes 12582912 | tf_op jit(solution)/shard_map/pallas_call | solution.py:1292
  251.8 1.4 slice_reduce_fusion
  253.1 1.0 reduce_sum.28
  254.1 0.9 slice.29
  256.8 1.3 slice.28
  258.1 1.0 fusion.9
  259.8 1.7 convolution_bitcast_fusion
  261.5 1.1 copy.48
  263.0 2.7 copy.47
  265.6 1.7 convert_element_type.39
  267.4 1.7 convert_element_type.40
  269.1 2.0 copy.84
  (41 shorter events, 7.8 us)
Async XLA Ops:
  0.6 17.4 %copy-start.4 = (bf16[128,4,1024]{2,1,0:T(4,128)(2,1)S(1)}, bf16[128,4,1024]{2,1,0:T(4,128)(2,1)}, u32[]{:S(2)}) copy-start(bf16[128,4,1024]{2,1,0:T(4,128)(2,1)} %param.16) | copy-start | bytes 3145732
  1.4 17.9 %copy-start.6 = (f32[4]{0:T(128)}, f32[4]{0:T(128)S(1)}, u32[]{:S(2)}) copy-start(f32[4]{0:T(128)S(1)} %compare_convert_fusion) | copy-start | bytes 52
  19.3 238.8 %copy-start.5 = (f32[4,3,1024]{2,0,1:T(4,128)S(1)}, f32[4,3,1024]{2,0,1:T(4,128)}, u32[]{:S(2)}) copy-start(f32[4,3,1024]{2,0,1:T(4,128)} %constant_dynamic-slice_fusion) | copy-start | bytes 147460
  19.3 238.8 %copy-start.7 = (f32[4]{0:T(128)S(1)}, f32[4]{0:T(128)}, u32[]{:S(2)}) copy-start(f32[4]{0:T(128)} %copy-done.6) | copy-start | bytes 52
  19.3 238.8 %copy-start.8 = (f32[3]{0:T(128)S(1)}, f32[3]{0:T(128)}, u32[]{:S(2)}) copy-start(f32[3]{0:T(128)} %param.28) | copy-start | bytes 40
  251.7 11.0 %copy-start.3 = (bf16[4,128,1024]{2,1,0:T(8,128)(2,1)S(1)}, bf16[4,128,1024]{2,1,0:T(8,128)(2,1)}, u32[]{:S(2)}) copy-start(bf16[4,128,1024]{2,1,0:T(8,128)(2,1)} %get-tuple-element.23) | copy-start | bytes 3145732
  261.5 4.1 %copy-start.2 = (bf16[9,128,512]{2,1,0:T(8,128)(2,1)S(1)}, bf16[9,128,512]{2,1,0:T(8,128)(2,1)}, u32[]{:S(2)}) copy-start(bf16[9,128,512]{2,1,0:T(8,128)(2,1)} %get-tuple-element.25) | copy-start | bytes 3538948
  262.9 4.4 %copy-start.1 = (bf16[9,128,512]{2,1,0:T(8,128)(2,1)S(1)}, bf16[9,128,512]{2,1,0:T(8,128)(2,1)}, u32[]{:S(2)}) copy-start(bf16[9,128,512]{2,1,0:T(8,128)(2,1)} %get-tuple-element.26) | copy-start | bytes 3538948
  265.6 3.5 %copy-start = (bf16[128,4,4096]{2,1,0:T(4,128)(2,1)S(1)}, bf16[128,4,4096]{2,1,0:T(4,128)(2,1)}, u32[]{:S(2)}) copy-start(bf16[128,4,4096]{2,1,0:T(4,128)(2,1)} %get-tuple-element.78) | copy-start | bytes 12582916

commit v3 on v2

--- a/solution.py
+++ b/solution.py
@@ -421,11 +421,11 @@
 
 def block_kernel(gains, pack, x_in, own1, own2, feat_grad, plain, order_back, order, style_weight, shared,
                  raised_out, conv_out, feat_natural, full1_out, arrived, x_out, scaled_one_out, by_image, feat_all,
-                 feat_out, back_all, grad1_out, grad2_out, color_in, every, every_shared, latent_grad,
+                 feat_out, back_all, grad1_out, grad2_out, color_in, style_out, sums_all, shared_sum, latent_grad,
                  demod1, demod2, color, rgb_grad, cols, rows_ref, noise, color_phases, packs, stacked,
                  full1, full2, copies, tile, grad_tile, field, total, back,
                  core1, core2, first1, first2, quad1, quad2, zsum1, zsum2, zin1, zin2, out1, out2,
-                 sums2, sums1, sums0, inner2, inner1, style_sums, vectors, owned, latent_in, raw,
+                 sums2, sums1, sums0, inner2, inner1, style_sums, vectors, owned, latent_in, raw, every, every_shared,
                  load_sem, store_sem, tile_sem, pack_send, pack_recv, x_send, x_recv, w_send, w_recv,
                  swap_send, swap_recv, grad_send, grad_recv, feat_send, feat_recv, back_send, back_recv,
                  core_send, core_recv, quad_send, quad_recv, z_send, z_recv, across_send, across_recv, twin_send, twin_recv,
@@ -1174,6 +1174,22 @@
             join_beside(0, 0)
     join_depth(0, 2)
     join_beside(0, 1)
+
+    for item in shared_moves + every_moves:
+        item.wait_recv()
+    sums_all[...] = sum(every[r, b] for r in range(8) for b in range(4))
+    shared_sum[...] = sum(every_shared[r] for r in range(8))
+    latents = jnp.concatenate([every_shared[r, 0:4, :] for r in range(8)], axis=0)
+    style_stores = []
+    for j in range(3):
+        value = jnp.concatenate([every[r, b, j : j + 1, :] for r in range(8) for b in range(4)], axis=0)
+        total[0, :, j * 128 : (j + 1) * 128] = lax.dot_general(
+            latents, value, (((0,), (0,)), ((), ())), precision=precise, preferred_element_type=F32
+        )
+        style_stores.append(
+            pltpu.make_async_copy(total.at[0, :, j * 128 : (j + 1) * 128], style_out.at[j], load_sem.at[6 + j])
+        )
+        style_stores[j].start()
     for g in range(3):
         twin_move(1, g).wait()
     store2 = pltpu.make_async_copy(out2, grad2_out, load_sem.at[1])
@@ -1200,8 +1216,10 @@
             beside_move(c, g).wait_send()
     for item in feat_moves:
         item.wait_send()
-    for item in back_moves + shared_moves + every_moves + color_moves:
+    for item in back_moves + color_moves + style_stores:
         item.wait()
+    for item in shared_moves + every_moves:
+        item.wait_send()
     for item in owned_moves + latent_moves:
         item.wait_send()
     for j in range(4):
@@ -1269,7 +1287,7 @@
         (field, F32), (field, F32), ((channels, pixels), BF), (wide_weight, BF), ((channels, pixels), BF),
         ((channels, half_pix), BF), ((channels, half_pix), BF), ((channels, pixels), BF), ((channels, pixels), BF),
         (feat_grad.shape, BF), ((4, local_ch, half_pix), BF), ((9, local_ch, channels), BF),
-        ((9, local_ch, channels), BF), ((4, 8, pixels // 4), F32), ((8, 4, 16, 128), F32), ((8, 8, 512), F32),
+        ((9, local_ch, channels), BF), ((4, 8, pixels // 4), F32), (style_weight.shape, F32), ((16, 128), F32), ((8, 512), F32),
         ((8, 512), F32),
     )
     vector = ((channels, 128), F32)
@@ -1284,6 +1302,7 @@
         ((9, local_ch, channels), BF), ((9, local_ch, channels), BF),
         ((3, channels, 128), F32), ((4, channels, 128), F32), vector, vector, vector, ((2, 8, channels), F32),
         ((4, 16, 128), F32), ((4, 16, 128), F32), ((4, 8, 512), F32), ((2, local_ch, 4, 512), BF),
+        ((8, 4, 16, 128), F32), ((8, 8, 512), F32),
     )
     counts = (
         [(10,), (5,), (2, 2)] + [(3,)] * 4 + [(2, 4)] * 2 + [(2, 6)] * 2 + [(4, 3)] * 2 + [(3,)] * 4
@@ -1292,14 +1311,14 @@
     results = pl.pallas_call(
         block_kernel,
         in_specs=[SMEM] + [ANY] * 5 + [vmem] * 3 + [ANY, vmem],
-        out_specs=[ANY] * 14 + [vmem] * 3,
+        out_specs=[ANY] * 15 + [vmem] * 3,
         out_shape=[jax.ShapeDtypeStruct(shape, dtype) for shape, dtype in outs],
         scratch_shapes=[pltpu.VMEM(shape, dtype) for shape, dtype in scratch]
         + [pltpu.SemaphoreType.DMA(count) for count in counts],
         compiler_params=pltpu.CompilerParams(vmem_limit_bytes=LIMIT, collective_id=0, has_side_effects=True),
         cost_estimate=pl.CostEstimate(flops=int(150e9), bytes_accessed=12 << 20, transcendentals=0),
     )(gains, pack, x_by_image, conv_first, conv_second, feat_grad, plain, order.T, order, style_weight, shared)
-    feat_out, back_all, grad_one, grad_two, color_in, every, every_shared, latent_grad = results[9:]
+    feat_out, back_all, grad_one, grad_two, color_in, style_weight_grad, summed, shared_sum, latent_grad = results[9:]
     feat_in_grad = back_all.transpose(1, 0, 2).astype(F32)
     grad_one, grad_two = grad_one.astype(F32), grad_two.astype(F32)
 
@@ -1322,8 +1341,6 @@
         precision=precise,
     ).reshape(images, 3, half_pix)
 
-    summed = jnp.sum(every, axis=(0, 1))
-    style_weight_grad = jnp.einsum("gbw,gbjc->jwc", every_shared[:, :4], every[:, :, :3], precision=precise)
     return (
         feat_out,
         rgb_out,
@@ -1336,7 +1353,7 @@
         summed[:3],
         summed[8:11],
         summed[3:5],
-        jnp.sum(every_shared[:, 4, :3], axis=0),
+        shared_sum[4, :3],
         summed[5:7, 0],
     )
 

time: 276 us -> 275 us (level)
  no operation moved by 1% of the time
where the time goes in v3:
time: 275 us; the launch traced here: 271 us
  Pallas kernels  232 us (84%)
  local copies, waits for them, and re-layouts  20 us (7%)
  other arithmetic  12.8 us (5%)
  matrix products  3.57 us (1%)
    pallas_call x1, Pallas kernels, image_body(): pl.pallas_call(block_kernel, in_specs=[SMEM] + [ANY] * 5 + [vmem] * 3 + [...  232 us
    unnamed x23, local copies, waits for them, and re-layouts  7.53 us

profile of v3, /device:TPU:0, one launch (start us, length us, event | category | flops | bytes accessed | tf_op | source)
XLA Modules:
  0.0 270.6 jit_solution(18357622494035331055)
XLA Ops:
  1.4 1.2 pad_maximum_fusion.2.gains
  3.4 1.6 fusion.15
  7.1 0.9 constant_dynamic-slice_fusion.1
  8.0 1.0 constant_dynamic-slice_fusion.3
  9.7 0.9 reshape.186
  11.1 0.8 fusion.6
  12.8 1.1 fusion.71
  13.9 1.3 pad_maximum_fusion.1.shared
  16.2 0.8 reshape.189
  16.9 1.1 fusion.1
  18.0 1.3 copy.68
  19.3 232.3 %shard_map.255 = (f32[4,512,1024]{2,1,0:T(8,128)}, f32[4,512,1024]{2,1,0:T(8,128)}, bf16[512,4096]{1,0:T(8,128)(2,1)}, bf16[9,512,512]{2,1,0:T(8,128)(2,1)}, bf1...) custom-call(f32[3]{0:T(128)} %pad_maximum_fusion.2.gains, ...), custom_call_target="tpu_custom_call" | custom-call | flops 149999992832 | bytes 12582912 | tf_op jit(solution)/shard_map/pallas_call | solution.py:1311
  251.6 1.3 slice_bitcast_fusion
  252.9 1.3 slice_reduce_fusion
  254.2 1.2 slice.25
  255.5 1.3 fusion.72
  256.7 1.3 slice.22
  258.1 1.0 fusion.9
  259.7 1.5 convert_bitcast_fusion
  261.2 2.7 copy.42
  263.9 1.7 convert_element_type.39
  265.6 1.7 convert_element_type.40
  267.3 2.0 copy.72
  269.3 0.9 copy.73
  (38 shorter events, 6.5 us)
Async XLA Ops:
  0.6 17.4 %copy-start.3 = (bf16[128,4,1024]{2,1,0:T(4,128)(2,1)S(1)}, bf16[128,4,1024]{2,1,0:T(4,128)(2,1)}, u32[]{:S(2)}) copy-start(bf16[128,4,1024]{2,1,0:T(4,128)(2,1)} %param.16) | copy-start | bytes 3145732
  1.4 17.9 %copy-start.6 = (f32[4]{0:T(128)}, f32[4]{0:T(128)S(1)}, u32[]{:S(2)}) copy-start(f32[4]{0:T(128)S(1)} %compare_convert_fusion) | copy-start | bytes 52
  19.3 238.7 %copy-start.5 = (f32[4,3,1024]{2,0,1:T(4,128)S(1)}, f32[4,3,1024]{2,0,1:T(4,128)}, u32[]{:S(2)}) copy-start(f32[4,3,1024]{2,0,1:T(4,128)} %constant_dynamic-slice_fusion) | copy-start | bytes 147460
  19.3 238.7 %copy-start.7 = (f32[4]{0:T(128)S(1)}, f32[4]{0:T(128)}, u32[]{:S(2)}) copy-start(f32[4]{0:T(128)} %copy-done.6) | copy-start | bytes 52
  19.3 238.7 %copy-start.8 = (f32[3]{0:T(128)S(1)}, f32[3]{0:T(128)}, u32[]{:S(2)}) copy-start(f32[3]{0:T(128)} %param.28) | copy-start | bytes 40
  251.6 12.2 %copy-start.2 = (bf16[9,128,512]{2,1,0:T(8,128)(2,1)S(1)}, bf16[9,128,512]{2,1,0:T(8,128)(2,1)}, u32[]{:S(2)}) copy-start(bf16[9,128,512]{2,1,0:T(8,128)(2,1)} %get-tuple-element.26) | copy-start | bytes 3538948
  261.2 4.4 %copy-start.1 = (bf16[9,128,512]{2,1,0:T(8,128)(2,1)S(1)}, bf16[9,128,512]{2,1,0:T(8,128)(2,1)}, u32[]{:S(2)}) copy-start(bf16[9,128,512]{2,1,0:T(8,128)(2,1)} %get-tuple-element.27) | copy-start | bytes 3538948
  263.9 3.5 %copy-start = (bf16[128,4,4096]{2,1,0:T(4,128)(2,1)S(1)}, bf16[128,4,4096]{2,1,0:T(4,128)(2,1)}, u32[]{:S(2)}) copy-start(bf16[128,4,4096]{2,1,0:T(4,128)(2,1)} %get-tuple-element.80) | copy-start | bytes 12582916
  267.3 2.0 copy-start.4
